TPU v7x, 32 devices: a whole 2x2x4 slice. The times are simulated.
32 devices in a mesh: node: 4 (over z), dev: 8 (over y, x, core).
Axes of the slice: x: 2, y: 2, z: 4, core: 2. Of those that a mesh axis runs over, the one named last changes fastest.
Arguments:
- amps: float32 [4, 8, 8, 1024], P('node', 'dev'), may hold values from -6 to 6
- amp_tile: int32 [4, 8], replicated, may hold values from 0 to 7, each once within a row
- ints: float32 [4, 8, 1024, 1024], P('node', 'dev'), may hold values from -0.1875 to 0.1875
- tasks: int32 [4, 16, 2], replicated, may hold values from 0 to 7, as said below
- pair_energy: float32 [4, 8], P('node', 'dev'), may hold values from -3 to -1
- virt_energy: float32 [4, 1024], replicated, may hold values from 0.5 to 3
Outputs:
- resid: float32 [4, 8, 4096], P('node', 'dev')
Inputs may be any that keep to these rules, and one draw needn't show every extreme that they name: Each row amp_tile[n] is a permutation of the 8 contracted tile pairs. `tasks`: the first column names an output tile pair below 4, the second a contracted tile pair below 8; the (ab, cd) pairs of one pair block are distinct.
All inputs are finite; a program needn't handle non-finite values.
Results may differ from a plain program's by a relative error of at most 0.0003.
Values sent between devices are 32-bit elements; how exact they have to be, the bound alone decides.
No kernel may reach another device: no remote copies, remote signals or barrier semaphores. Data moves between devices by JAX's collectives and lax.ppermute only.
A program may use at most 64 MiB of HBM per device.

v0:
```python
import jax
import jax.numpy as jnp
from jax import lax
from jax.sharding import PartitionSpec as P


def tile_product(left, right):
    return lax.dot_general(
        left,
        right,
        (((1,), (1,)), ((), ())),
        precision=lax.Precision.HIGHEST,
        preferred_element_type=jnp.float32,
    )


def on_device(amps, amp_tile, ints, tasks, pair_energy, virt_energy):
    my_dev = lax.axis_index("dev")
    my_node = lax.axis_index("node")
    pairs = amps.shape[2]
    width = amps.shape[3]
    block_count = amp_tile.shape[0]
    my_slots = lax.dynamic_index_in_dim(amp_tile, my_node, 0, keepdims=False)
    wanted = my_slots == my_dev
    my_amp = jnp.sum(
        jnp.where(wanted[:, None, None], lax.all_gather(amps, "dev", axis=1, tiled=True)[0], 0.0),
        axis=0,
    )
    hit_mask = (tasks[:, :, 0] == my_node) & (tasks[:, :, 1] == my_dev)
    hits = jnp.sum(hit_mask.astype(jnp.int32), axis=1)
    my_tile = ints[0, 0]
    piece = lax.all_gather(my_amp[None], "node", axis=0, tiled=True)

    def one_block(position, acc):
        amp_block = lax.dynamic_index_in_dim(piece, position, 0, keepdims=False)

        def add_term(inner):
            current = lax.dynamic_slice(inner, (position, 0, 0), (1, pairs, width))
            update = current + tile_product(amp_block, my_tile)[None]
            return lax.dynamic_update_slice(inner, update, (position, 0, 0))

        return lax.cond(hits[position] > 0, add_term, lambda inner: inner, acc)

    partial_ladder = lax.fori_loop(
        0, piece.shape[0], one_block, jnp.zeros((block_count, pairs, width), jnp.float32)
    )
    moved = lax.all_to_all(partial_ladder, "node", split_axis=0, concat_axis=2, tiled=True)
    ladder = lax.psum_scatter(moved, "dev", scatter_dimension=1, tiled=True)
    denominator = pair_energy[:, :, None] - virt_energy.reshape(1, 1, -1)
    return ladder / denominator


def solution(mesh):
    in_specs = (
        P("node", "dev", None, None),
        P(),
        P("node", "dev", None, None),
        P(),
        P("node", "dev"),
        P(),
    )
    out_specs = P("node", "dev", None)
    return jax.shard_map(
        on_device, mesh=mesh, in_specs=in_specs, out_specs=out_specs, check_vma=False
    )
```

profile of v0, /device:TPU:0, one launch (start us, length us, event | category | flops | bytes accessed | tf_op | source)
XLA Modules:
  0.0 128.9 jit_solution(7397356067534582724)
XLA Ops:
  6.5 11.0 %all_gather.6 = f32[1,8,8,1024]{3,2,0,1:T(8,128)S(1)} all-gather(f32[1,1,8,1024]{3,2,0,1:T(8,128)} %bitcast.35), channel_id=1, replica_groups=mesh['node'=4,'dev'=8] {'dev'}, dimensions={1}, use_global_device_ids=true | all-gather | bytes 294912 | tf_op jit(solution)/shard_map/all_gather | solution.py:26
  17.5 0.7 compare_bitcast_fusion
  18.2 0.1 fusion.5
  18.3 13.6 %all-gather = f32[32,1024]{1,0:T(8,128)S(1)} all-gather(f32[8,1024]{1,0:T(8,128)S(1)} %fusion.5), channel_id=2, replica_groups=mesh['node'=4,'dev'=8] {'node'}, dimensions={0}, use_global_device_ids=true | all-gather | bytes 163840 | tf_op jit(solution)/shard_map/all_gather | solution.py:32
  31.9 0.9 fusion.6
  32.8 0.7 broadcast_in_dim.24
  33.4 0.0 copy-start.1
  33.4 0.0 copy-start.2
  33.4 23.9 %while.16 = (s32[]{:T(128)}, f32[4,8,1024]{2,1,0:T(8,128)}, s32[4]{0:T(128)S(1)}, f32[4,8,1024]{2,1,0:T(8,128)S(1)}, f32[1024,1024]{1,0:T(8,128)}, /*index=5*/s32[]{:T(128)}, s32[1]{0:T(128)}) while((s32[]{:T(128)}, f32[4,8,1024]{2,1,0:T(8,128)}, s32[4]{0:T(128)S(1)}, f32[4,8,1024]{2,1,0:T(8,128)S(1)}, f32[1024,1024]{1,0:T(8,128)}, ...), condition=%wide.region_5.6_spmd, body=%wide.region_2.5_spmd.sunk | while | flops 100671488 | bytes 4293301 | solution.py:44
  33.5 0.6 dynamic_slice.34
  34.7 6.3 %conditional.2 = (f32[4,8,1024]{2,1,0:T(8,128)}) conditional(s32[]{:T(128)} %bitcast.30, f32[4,8,1024]{2,1,0:T(8,128)} %get-tuple-element.183, (s32[]{:T(128)}, f32[4,8,1024]{2,1,0:T(8,128)}, f32[4,8,1024]{2,1,0:T(8,128)S(1)}, f32[1024,1024]{1,0:T(8,128)}) %tuple.41), branch_computations={%region_3.3_spmd, %region_4.4_spmd} | conditional | flops 100671488 | bytes 4293166 | solution.py:42
  34.7 6.3 %fusion.1 = f32[4,8,1024]{2,1,0:T(8,128)} fusion(f32[4,8,1024]{2,1,0:T(8,128)} %get-tuple-element.122, s32[]{:T(128)S(6)} %select_n.17, f32[1024,1024]{1,0:T(8,128)} %get-tuple-element.125, f32[4,8,1024]{2,1,0:T(8,128)S(1)} %get-tuple-element.124, s32[]{:T(128)} %get-tuple-element.123), kind=kOutput, calls=%fused_computation.2 | convolution fusion | flops 100671488 | bytes 4293124 | tf_op jit(solution)/shard_map/while/body/eval_jaxpr/cond/branch_1_fun/dot_general | solution.py:8
  41.0 0.6 dynamic_slice.34
  42.3 6.3 %conditional.2 = (f32[4,8,1024]{2,1,0:T(8,128)}) conditional(s32[]{:T(128)} %bitcast.30, f32[4,8,1024]{2,1,0:T(8,128)} %get-tuple-element.183, (s32[]{:T(128)}, f32[4,8,1024]{2,1,0:T(8,128)}, f32[4,8,1024]{2,1,0:T(8,128)S(1)}, f32[1024,1024]{1,0:T(8,128)}) %tuple.41), branch_computations={%region_3.3_spmd, %region_4.4_spmd} | conditional | flops 100671488 | bytes 4293166 | solution.py:42
  42.3 6.3 %fusion.1 = f32[4,8,1024]{2,1,0:T(8,128)} fusion(f32[4,8,1024]{2,1,0:T(8,128)} %get-tuple-element.122, s32[]{:T(128)S(6)} %select_n.17, f32[1024,1024]{1,0:T(8,128)} %get-tuple-element.125, f32[4,8,1024]{2,1,0:T(8,128)S(1)} %get-tuple-element.124, s32[]{:T(128)} %get-tuple-element.123), kind=kOutput, calls=%fused_computation.2 | convolution fusion | flops 100671488 | bytes 4293124 | tf_op jit(solution)/shard_map/while/body/eval_jaxpr/cond/branch_1_fun/dot_general | solution.py:8
  48.6 0.6 dynamic_slice.34
  49.8 6.3 %conditional.2 = (f32[4,8,1024]{2,1,0:T(8,128)}) conditional(s32[]{:T(128)} %bitcast.30, f32[4,8,1024]{2,1,0:T(8,128)} %get-tuple-element.183, (s32[]{:T(128)}, f32[4,8,1024]{2,1,0:T(8,128)}, f32[4,8,1024]{2,1,0:T(8,128)S(1)}, f32[1024,1024]{1,0:T(8,128)}) %tuple.41), branch_computations={%region_3.3_spmd, %region_4.4_spmd} | conditional | flops 100671488 | bytes 4293166 | solution.py:42
  49.8 6.3 %fusion.1 = f32[4,8,1024]{2,1,0:T(8,128)} fusion(f32[4,8,1024]{2,1,0:T(8,128)} %get-tuple-element.122, s32[]{:T(128)S(6)} %select_n.17, f32[1024,1024]{1,0:T(8,128)} %get-tuple-element.125, f32[4,8,1024]{2,1,0:T(8,128)S(1)} %get-tuple-element.124, s32[]{:T(128)} %get-tuple-element.123), kind=kOutput, calls=%fused_computation.2 | convolution fusion | flops 100671488 | bytes 4293124 | tf_op jit(solution)/shard_map/while/body/eval_jaxpr/cond/branch_1_fun/dot_general | solution.py:8
  56.1 0.6 dynamic_slice.34
  57.4 4.8 %all-to-all-start = ((f32[4,8,1024]{2,1,0:T(8,128)}), f32[4,8,1024]{2,1,0:T(8,128)S(1)}, u32[]{:S(2)}, u32[]{:S(2)}) async-start(f32[4,8,1024]{2,1,0:T(8,128)} %get-tuple-element.133), calls=%async_computation | async-start | bytes 262144 | tf_op jit(solution)/shard_map/all_to_all | solution.py:47
  62.1 0.0 all-reduce.3.cloned.1.call-start
  62.8 5.3 %all-to-all-done = f32[4,8,1024]{2,1,0:T(8,128)S(1)} async-done(((f32[4,8,1024]{2,1,0:T(8,128)}), f32[4,8,1024]{2,1,0:T(8,128)S(1)}, u32[]{:S(2)}, u32[]{:S(2)}) %all-to-all-start) | async-done | bytes 131104 | tf_op jit(solution)/shard_map/all_to_all | solution.py:47
  68.1 0.0 copy-start
  68.1 0.6 copy-done
  68.7 0.0 all-reduce.3.cloned.1.call-update
  68.7 0.0 copy-done.1
  68.8 0.0 copy-done.2
  68.8 0.7 dynamic-slice
  69.5 50.4 %all-reduce.3.cloned.1.call-done = f32[1,8,4096]{2,1,0:T(8,128)} async-done(((f32[1,8,4096]{2,1,0:T(8,128)}), f32[1,8,4096]{2,1,0:T(8,128)}) %all-reduce.3.cloned.1.call-update) | async-done | bytes 131088
  119.9 2.2 %dynamic-slice_divide_fusion = f32[1,1,4096]{2,1,0:T(1,128)} fusion(f32[1,1,4096]{2,1,0:T(1,128)S(1)} %sub.24, f32[1,8,4096]{2,1,0:T(8,128)} %all-reduce.3.cloned.1.call-done, u32[]{:T(128)} %bitcast.16), kind=kLoop, calls=%fused_computation.8 | loop fusion | flops 4096 | bytes 49156 | tf_op jit(solution)/shard_map/div | solution.py:50
  (3 shorter events, 0.0 us)
Async XLA Ops:
  33.4 35.3 %copy-start.1 = (f32[4,1024]{1,0:T(4,128)S(1)}, f32[4,1024]{1,0:T(4,128)}, u32[]{:S(2)}) copy-start(f32[4,1024]{1,0:T(4,128)} %param.15) | copy-start | bytes 49156
  33.4 35.4 %copy-start.2 = (u32[32]{0:T(128)S(1)}, u32[32]{0:T(128)}, u32[]{:S(2)}) copy-start(u32[32]{0:T(128)} %constant.58) | copy-start | bytes 388
  57.4 10.7 %all-to-all-start = ((f32[4,8,1024]{2,1,0:T(8,128)}), f32[4,8,1024]{2,1,0:T(8,128)S(1)}, u32[]{:S(2)}, u32[]{:S(2)}) async-start(f32[4,8,1024]{2,1,0:T(8,128)} %get-tuple-element.133), calls=%async_computation | async-start | bytes 262144 | tf_op jit(solution)/shard_map/all_to_all | solution.py:47
  62.1 57.7 %all-reduce.3.cloned.1.call-start = ((), (), s32[]{:S(2)}) async-start(), calls=%async_computation.1 | async-start | bytes 262144
  68.1 0.6 copy-start
Sparse Core Ops, SparseCore 0:
  68.9 50.9 all-reduce.2
where the time goes:
time: 131 us; the launch traced here: 129 us
  waiting for transfers between devices  55.7 us (43%)
  blocking collectives  24.5 us (19%)
  matrix products  18.9 us (14%)
  between operations  14.1 us (11%)
  starting transfers between devices  4.75 us (4%)
  local copies, waits for them, and re-layouts  4.44 us (3%)
  other arithmetic  3.93 us (3%)
  loops' own time  2.65 us (2%)
    unnamed x2, waiting for transfers between devices  50.4 us
    dot_general x3, matrix products, tile_product(): lax.dot_general(left, right, (((1,), (1,)), ((), ())), precision=lax.Prec...  18.9 us
    all_gather x1, blocking collectives, on_device(): piece = lax.all_gather(my_amp[None], 'node', axis=0, tiled=True)  13.6 us
    all_gather x1, blocking collectives, on_device(): lax.all_gather(amps, 'dev', axis=1, tiled=True)[0]  11 us
    all_to_all x1, waiting for transfers between devices, on_device(): lax.all_to_all(partial_ladder, 'node', split_axis=0, concat_axis=2, tiled...  5.27 us
    all_to_all x1, starting transfers between devices, on_device(): lax.all_to_all(partial_ladder, 'node', split_axis=0, concat_axis=2, tiled...  4.75 us
  transfers between devices with their start and end apart: 2, of which 2 were waited for; matrix products, arithmetic and copies ran while one was open for 1% of the time, Pallas kernels for 0%

commit v1 on v0

v1 whole, which is shorter than its diff:
```python
import jax
import jax.numpy as jnp
from jax import lax
from jax.sharding import PartitionSpec as P


def on_device(amps, amp_tile, ints, tasks, pair_energy, virt_energy):
    nodes, devs = lax.axis_size("node"), lax.axis_size("dev")
    my_node, my_dev = lax.axis_index("node"), lax.axis_index("dev")
    pairs, width = amps.shape[2], amps.shape[3]

    slots = lax.all_gather(amps[0, 0], "dev", axis=0)
    wanted = lax.dynamic_index_in_dim(amp_tile, my_node, 0, keepdims=False) == my_dev
    mine = jnp.sum(jnp.where(wanted[:, None, None], slots, 0.0), axis=0)

    arrived = [mine] + [
        lax.ppermute(mine, "node", [(i, i ^ k) for i in range(nodes)])
        for k in range(1, nodes)
    ]
    blocks = my_node ^ jnp.arange(nodes, dtype=jnp.int32)
    hit = jnp.any((tasks[:, :, 0] == my_node) & (tasks[:, :, 1] == my_dev), axis=1)
    stacked = jnp.stack(arrived)
    ordered = jnp.stack(
        [lax.dynamic_index_in_dim(stacked, blocks[k], 0, keepdims=False) for k in range(nodes)]
    )
    ordered = jnp.where(hit[:, None, None], ordered, 0.0)
    products = lax.dot_general(
        ordered.reshape(nodes * pairs, width),
        ints[0, 0],
        (((1,), (1,)), ((), ())),
        precision=lax.Precision.HIGH,
        preferred_element_type=jnp.float32,
    )

    terms = lax.all_to_all(products, ("node", "dev"), 0, 0, tiled=True)
    ladder = jnp.sum(terms.reshape(nodes, devs, width), axis=1)
    resid = ladder / (pair_energy - virt_energy)
    return resid.reshape(1, 1, nodes * width)


def solution(mesh):
    in_specs = (
        P("node", "dev", None, None),
        P(),
        P("node", "dev", None, None),
        P(),
        P("node", "dev"),
        P(),
    )
    return jax.shard_map(
        on_device, mesh=mesh, in_specs=in_specs, out_specs=P("node", "dev", None), check_vma=False
    )
```

time: 131 us -> 44.9 us (0.34); the launches traced: 129 us -> 44.4 us
  waiting for transfers between devices: 55.7 us -> 7.59 us
  matrix products: 18.9 us -> 4.15 us
  blocking collectives: 24.5 us -> 11.1 us
  between operations: 14.1 us -> 8.32 us
  starting transfers between devices: 4.75 us -> 9.32 us
  loops' own time: 2.65 us -> 0 us
  local copies, waits for them, and re-layouts: 4.44 us -> 2.11 us
  other arithmetic: 3.93 us -> 1.79 us
    unnamed x2 -> x0, waiting for transfers between devices: 50.4 us -> none
    dot_general x3 -> x1, matrix products: 18.9 us -> 4.15 us  [on_device(): lax.dot_general(ordered.reshape(nodes * pairs, width), ints[0, 0], (((1,)...]
    all_gather x2 -> x1, blocking collectives: 24.5 us -> 11.1 us  [on_device(): slots = lax.all_gather(amps[0, 0], 'dev', axis=0)]
    ppermute x0 -> x3, starting transfers between devices: none -> 4.45 us  [on_device(): lax.ppermute(mine, 'node', [(i, i ^ k) for i in range(nodes)])]
    another operation x5 -> x0, loops' own time: 2.65 us -> none  [the longest x1 2.58 us: on_device(): lax.fori_loop(0, piece.shape[0], one_block, jnp.zeros((block_count, pairs...]
    dynamic_slice x4 -> x1, local copies, waits for them, and re-layouts: 2.43 us -> 0.02 us  [on_device(): lax.dynamic_index_in_dim(stacked, blocks[k], 0, keepdims=False)]
    all_to_all x1, waiting for transfers between devices: 5.27 us -> 7.58 us  [on_device(): terms = lax.all_to_all(products, ('node', 'dev'), 0, 0, tiled=True)]
    div x1, other arithmetic: 2.22 us -> 0.01 us  [on_device(): resid = ladder / (pair_energy - virt_energy)]
  transfers between devices with their start and end apart: 2 -> 4, of which waited for: 2 -> 1; matrix products, arithmetic and copies ran while one was open for 1% -> 4% of each run, Pallas kernels for 0% -> 0%
where the time goes in v1:
time: 44.9 us; the launch traced here: 44.4 us
  blocking collectives  11.1 us (25%)
  starting transfers between devices  9.32 us (21%)
  between operations  8.32 us (19%)
  waiting for transfers between devices  7.59 us (17%)
  matrix products  4.15 us (9%)
  local copies, waits for them, and re-layouts  2.11 us (5%)
  other arithmetic  1.79 us (4%)
    all_gather x1, blocking collectives, on_device(): slots = lax.all_gather(amps[0, 0], 'dev', axis=0)  11.1 us
    all_to_all x1, waiting for transfers between devices, on_device(): terms = lax.all_to_all(products, ('node', 'dev'), 0, 0, tiled=True)  7.58 us
    all_to_all x1, starting transfers between devices, on_device(): terms = lax.all_to_all(products, ('node', 'dev'), 0, 0, tiled=True)  4.87 us
    ppermute x3, starting transfers between devices, on_device(): lax.ppermute(mine, 'node', [(i, i ^ k) for i in range(nodes)])  4.45 us
    dot_general x1, matrix products, on_device(): lax.dot_general(ordered.reshape(nodes * pairs, width), ints[0, 0], (((1,)...  4.15 us
    reduce_or x1, other arithmetic, on_device(): jnp.any((tasks[:, :, 0] == my_node) & (tasks[:, :, 1] == my_dev), axis=1)  0.92 us
  transfers between devices with their start and end apart: 4, of which 1 were waited for; matrix products, arithmetic and copies ran while one was open for 4% of the time, Pallas kernels for 0%

profile of v1, /device:TPU:0, one launch (start us, length us, event | category | flops | bytes accessed | tf_op | source)
XLA Modules:
  0.0 44.4 jit_solution(2559210590856192151)
XLA Ops:
  0.0 0.0 copy-start
  0.0 11.1 %all-gather = f32[8,1,8,1024]{3,2,1,0:T(8,128)S(1)} all-gather(f32[1,1,8,1024]{3,2,1,0:T(8,128)} %param.6), channel_id=2, replica_groups=mesh['node'=4,'dev'=8] {'dev'}, dimensions={0}, use_global_device_ids=true | all-gather | bytes 294912 | tf_op jit(solution)/shard_map/all_gather | solution.py:12
  11.1 0.7 %compare_bitcast_fusion = pred[8]{0:T(512)(128)(4,1)S(1)} fusion(s32[4,8]{1,0:T(4,128)} %param.7, s32[]{:T(128)S(6)} %select_n.35, s32[]{:T(128)S(6)} %axis_index.25), kind=kLoop, calls=%fused_computation.19 | loop fusion | flops 8 | bytes 48 | tf_op jit(solution)/shard_map/eq | solution.py:13
  11.8 0.1 fusion.5
  11.9 1.6 %collective-permute-start = (f32[8,1024]{1,0:T(8,128)S(1)}, f32[8,1024]{1,0:T(8,128)S(1)}, u32[]{:S(2)}, u32[]{:S(2)}) collective-permute-start(f32[8,1024]{1,0:T(8,128)S(1)} %fusion.5), channel_id=1, source_target_pairs={{0,8},{8,0},{16,24},{24,16},{1,9},{9,1},{17,25},{25,17},{2,10},{10... | collective-permute-start | bytes 98312 | tf_op jit(solution)/shard_map/ppermute | solution.py:17
  13.5 2.6 %collective-permute-start.1 = (f32[8,1024]{1,0:T(8,128)S(1)}, f32[8,1024]{1,0:T(8,128)S(1)}, u32[]{:S(2)}, u32[]{:S(2)}) collective-permute-start(f32[8,1024]{1,0:T(8,128)S(1)} %fusion.5), channel_id=1, source_target_pairs={{0,16},{8,24},{16,0},{24,8},{1,17},{9,25},{17,1},{25,9},{2,18},{10... | collective-permute-start | bytes 98312 | tf_op jit(solution)/shard_map/ppermute | solution.py:17
  16.1 0.2 collective-permute-start.2
  16.3 0.9 %and_reduce_fusion = pred[4]{0:T(512)(128)(4,1)S(1)} fusion(s32[4,16,2]{1,2,0:T(2,128)} %param.9, s32[]{:T(128)S(6)} %axis_index.25, s32[]{:T(128)S(6)} %axis_index.23), kind=kLoop, calls=%fused_computation.18 | loop fusion | flops 252 | bytes 524 | tf_op jit(solution)/shard_map/reduce_or | solution.py:21
  17.3 0.7 %fusion.18 = (s32[1]{0:T(128)}, s32[1]{0:T(128)}, s32[1]{0:T(128)}, s32[1]{0:T(128)}) fusion(s32[4]{0:T(128)S(1)} %iota_xor_fusion), kind=kLoop, calls=%fused_computation.28 | loop fusion | bytes 32 | tf_op jit(solution)/shard_map/slice | solution.py:24
  25.5 0.0 collective-permute-done
  25.5 0.0 collective-permute-done.1
  25.5 0.0 collective-permute-done.2
  25.6 4.2 %fusion.2 = f32[32,1,1024]{2,0,1:T(8,128)S(1)} fusion(f32[1,1,1024,1024]{3,2,1,0:T(8,128)} %param.8, f32[1,8,1024]{2,1,0:T(8,128)S(1)} %get-tuple-element.6, f32[1,8,1024]{2,1,0:T(8,128)S(1)} %get-tuple-element.7, f32[1,8,1024]{2,1,0:T(8,128)S(1)} %get-tuple-element.8, f32[1,8,1024]{2,1,0:T(8,128)S(1)} %get-tuple-element.5, pred[4]{0:T(512)(128)(4,1)S(1)} %and_reduce_fusion), kind=kOutput, calls=%fused_computation.2 | convolution fusion | flops 201457664 | bytes 4456452 | tf_op jit(solution)/shard_map/dot_general | solution.py:27
  29.8 0.8 %copy.7 = f32[32,1,1024]{2,1,0:T(1,128)} copy(f32[32,1,1024]{2,0,1:T(8,128)S(1)} %fusion.2) | data formatting | bytes 262144 | tf_op jit(solution)/shard_map/all_to_all | solution.py:35
  30.5 4.9 %all-to-all-start = ((f32[32,1,1024]{2,1,0:T(1,128)}), f32[32,1,1024]{2,1,0:T(1,128)S(1)}, u32[]{:S(2)}, u32[]{:S(2)}) async-start(f32[32,1,1024]{2,1,0:T(1,128)} %copy.7), calls=%async_computation | async-start | bytes 262144 | tf_op jit(solution)/shard_map/all_to_all | solution.py:35
  36.1 7.6 %all-to-all-done = f32[32,1,1024]{2,1,0:T(1,128)S(1)} async-done(((f32[32,1,1024]{2,1,0:T(1,128)}), f32[32,1,1024]{2,1,0:T(1,128)S(1)}, u32[]{:S(2)}, u32[]{:S(2)}) %all-to-all-start) | async-done | bytes 131104 | tf_op jit(solution)/shard_map/all_to_all | solution.py:35
  43.6 0.1 bitcast_reduce_fusion
  43.7 0.0 copy-done
  43.7 0.6 %reshape.56 = f32[1,1,4096]{2,1,0:T(1,128)} reshape(f32[4,1024]{1,0:T(4,128)S(1)} %subtract_divide_fusion) | data formatting | bytes 32768 | tf_op jit(solution)/shard_map/reshape | solution.py:38
  (4 shorter events, 0.1 us)
Async XLA Ops:
  0.0 43.7 %copy-start = (f32[4,1024]{1,0:T(4,128)S(1)}, f32[4,1024]{1,0:T(4,128)}, u32[]{:S(2)}) copy-start(f32[4,1024]{1,0:T(4,128)} %param.11) | copy-start | bytes 49156
  11.9 13.7 %collective-permute-start = (f32[8,1024]{1,0:T(8,128)S(1)}, f32[8,1024]{1,0:T(8,128)S(1)}, u32[]{:S(2)}, u32[]{:S(2)}) collective-permute-start(f32[8,1024]{1,0:T(8,128)S(1)} %fusion.5), channel_id=1, source_target_pairs={{0,8},{8,0},{16,24},{24,16},{1,9},{9,1},{17,25},{25,17},{2,10},{10... | collective-permute-start | bytes 98312 | tf_op jit(solution)/shard_map/ppermute | solution.py:17
  13.5 12.0 %collective-permute-start.1 = (f32[8,1024]{1,0:T(8,128)S(1)}, f32[8,1024]{1,0:T(8,128)S(1)}, u32[]{:S(2)}, u32[]{:S(2)}) collective-permute-start(f32[8,1024]{1,0:T(8,128)S(1)} %fusion.5), channel_id=1, source_target_pairs={{0,16},{8,24},{16,0},{24,8},{1,17},{9,25},{17,1},{25,9},{2,18},{10... | collective-permute-start | bytes 98312 | tf_op jit(solution)/shard_map/ppermute | solution.py:17
  16.1 9.4 %collective-permute-start.2 = (f32[8,1024]{1,0:T(8,128)S(1)}, f32[8,1024]{1,0:T(8,128)S(1)}, u32[]{:S(2)}, u32[]{:S(2)}) collective-permute-start(f32[8,1024]{1,0:T(8,128)S(1)} %fusion.5), channel_id=1, source_target_pairs={{0,24},{8,16},{16,8},{24,0},{1,25},{9,17},{17,9},{25,1},{2,26},{10... | collective-permute-start | bytes 98312 | tf_op jit(solution)/shard_map/ppermute | solution.py:17
  30.5 13.1 %all-to-all-start = ((f32[32,1,1024]{2,1,0:T(1,128)}), f32[32,1,1024]{2,1,0:T(1,128)S(1)}, u32[]{:S(2)}, u32[]{:S(2)}) async-start(f32[32,1,1024]{2,1,0:T(1,128)} %copy.7), calls=%async_computation | async-start | bytes 262144 | tf_op jit(solution)/shard_map/all_to_all | solution.py:35

commit v2 on v1

v2 whole, which is shorter than its diff:
```python
import jax
import jax.numpy as jnp
from jax import lax
from jax.experimental import pallas as pl
from jax.experimental.pallas import tpu as pltpu
from jax.sharding import PartitionSpec as P

LANES = 128
VMEM_LIMIT = 24 * 2**20
CONTRACT_LAST = (((1,), (1,)), ((), ()))
MINE, THEIRS, HITS = 0, 1, 2
VMEM = pl.BlockSpec(memory_space=pltpu.VMEM)
HBM = pl.BlockSpec(memory_space=pltpu.HBM)
CHUNKS = 2


def call(kernel, name, out_shape, in_specs, scratch=(), flops=0, moved=0):
    return pl.pallas_call(
        kernel,
        out_shape=out_shape,
        in_specs=in_specs,
        out_specs=jax.tree.map(lambda _: VMEM, out_shape),
        scratch_shapes=list(scratch),
        compiler_params=pltpu.CompilerParams(vmem_limit_bytes=VMEM_LIMIT),
        cost_estimate=pl.CostEstimate(flops=flops, bytes_accessed=moved, transcendentals=0),
        name=name,
    )


def high_and_low(x):
    high = x.astype(jnp.bfloat16)
    return high, (x - high.astype(jnp.float32)).astype(jnp.bfloat16)


def split_rows(ints_hbm, first, land_ref, sems, high_ref, low_ref):
    chunks = sems.shape[0]
    rows = high_ref.shape[0] // chunks
    copies = [
        pltpu.make_async_copy(
            ints_hbm.at[pl.ds(first + i * rows, rows)], land_ref.at[pl.ds(i * rows, rows)], sems.at[i]
        )
        for i in range(chunks)
    ]
    for copy in copies:
        copy.start()

    def finish():
        for i, copy in enumerate(copies):
            copy.wait()
            part = pl.ds(i * rows, rows)
            high_ref[part, :], low_ref[part, :] = high_and_low(land_ref[part, :])

    return finish


def in_hbm(x):
    return pltpu.with_memory_space_constraint(x, pltpu.HBM)


def stage_kernel(
    tile_hbm, tasks_hbm, amps_hbm, ints_hbm,
    facts_ref, own_ref, high_ref, low_ref,
    tile_ref, tasks_ref, sems, land_ref, ints_sems,
):
    copies = [
        pltpu.make_async_copy(src, dst, sems.at[i])
        for i, (src, dst) in enumerate(
            [(tile_hbm, tile_ref), (tasks_hbm, tasks_ref), (amps_hbm, own_ref)]
        )
    ]
    for copy in copies:
        copy.start()
    finish = split_rows(ints_hbm, 0, land_ref, ints_sems, high_ref, low_ref)
    my_node, my_dev = lax.axis_index("node"), lax.axis_index("dev")
    nodes = tasks_ref.shape[0]
    for copy in copies:
        copy.wait()
    row = tile_ref[pl.ds(my_node, 1), :]
    position = lax.broadcasted_iota(jnp.int32, row.shape, 1)
    for where, owner in ((MINE, my_dev), (THEIRS, my_dev ^ 1)):
        slot = jnp.sum(jnp.where(row == owner, position, 0), axis=1, keepdims=True)
        facts_ref[where : where + 1, :] = jnp.broadcast_to(slot, (1, LANES))
    for k in range(nodes):
        task = tasks_ref[my_node ^ k]
        hit = jnp.where((task[0:1] == my_node) & (task[1:2] == my_dev), 1, 0)
        hit = jnp.max(hit, axis=1, keepdims=True)
        facts_ref[HITS + k : HITS + k + 1, :] = jnp.broadcast_to(hit, (1, LANES))
    finish()


def split_kernel(
    after_ref, pair_ref, virt_hbm, ints_hbm, denom_ref, high_ref, low_ref, virt_ref, sem, land_ref, ints_sems
):
    del after_ref
    copy = pltpu.make_async_copy(virt_hbm, virt_ref, sem)
    copy.start()
    finish = split_rows(
        ints_hbm, ints_hbm.shape[0] - high_ref.shape[0], land_ref, ints_sems, high_ref, low_ref
    )
    copy.wait()
    denom = pair_ref[0, 0] - virt_ref[...]
    for j in range(denom_ref.shape[1]):
        denom_ref[:, j, :] = denom[:, j * LANES : (j + 1) * LANES]
    finish()


def pick_kernel(facts_ref, *refs):
    pieces, (keep_ref, give_ref) = refs[:-2], refs[-2:]
    chip = lax.axis_index("dev") // 2
    for row, out_ref in ((MINE, keep_ref), (THEIRS, give_ref)):
        step = (facts_ref[row : row + 1, 0:1] // 2) ^ chip
        tile = pieces[0][...]
        for j, piece in enumerate(pieces[1:], 1):
            tile = jnp.where(step == j, piece[...], tile)
        out_ref[...] = tile


def merge_kernel(facts_ref, keep_ref, got_ref, mine_ref):
    core = lax.axis_index("dev") % 2
    mine_ref[...] = jnp.where(
        facts_ref[MINE : MINE + 1, 0:1] % 2 == core, keep_ref[...], got_ref[...]
    )


def product_kernel(facts_ref, high_a_ref, low_a_ref, high_b_ref, low_b_ref, *refs):
    pieces, out_ref, rows_ref = refs[:-2], refs[-2], refs[-1]
    my_node = lax.axis_index("node")
    pairs = pieces[0].shape[0]
    total = len(pieces) * pairs
    for k, piece in enumerate(pieces):
        start = pl.multiple_of((my_node ^ k) * pairs, pairs)
        hit = facts_ref[HITS + k : HITS + k + 1, 0:1]
        rows_ref[pl.ds(start, pairs), :] = jnp.where(hit > 0, piece[...], 0.0)
    amp_high, amp_low = high_and_low(rows_ref[...])
    amp_both = jnp.concatenate([amp_high, amp_low], axis=0)
    first = 0
    for high_ref, low_ref in ((high_a_ref, low_a_ref), (high_b_ref, low_b_ref)):
        both = lax.dot_general(
            amp_both, high_ref[...], CONTRACT_LAST, preferred_element_type=jnp.float32
        )
        rest = lax.dot_general(
            amp_high, low_ref[...], CONTRACT_LAST, preferred_element_type=jnp.float32
        )
        result = both[:total] + (both[total:] + rest)
        for j in range(high_ref.shape[0] // LANES):
            out_ref[:, first + j, :] = result[:, j * LANES : (j + 1) * LANES]
        first += high_ref.shape[0] // LANES


def on_device(amps, amp_tile, ints, tasks, pair_energy, virt_energy):
    nodes, devs = lax.axis_size("node"), lax.axis_size("dev")
    pairs, width = amps.shape[2], amps.shape[3]
    groups = width // LANES
    tile = jax.ShapeDtypeStruct((pairs, width), jnp.float32)
    task_rows = jnp.swapaxes(tasks, 1, 2)

    own = amps[0, 0]
    others = [
        lax.ppermute(own, "dev", [(i, i ^ k) for i in range(devs)]) for k in range(2, devs, 2)
    ]
    half = jax.ShapeDtypeStruct((width // 2, width), jnp.bfloat16)
    landing = [pltpu.VMEM(half.shape, jnp.float32), pltpu.SemaphoreType.DMA((CHUNKS,))]
    facts, own, high_a, low_a = call(
        stage_kernel,
        "stage",
        (
            jax.ShapeDtypeStruct((HITS + nodes, LANES), jnp.int32),
            tile,
            half,
            half,
        ),
        [HBM] * 4,
        [
            pltpu.VMEM(amp_tile.shape, jnp.int32),
            pltpu.VMEM(task_rows.shape, jnp.int32),
            pltpu.SemaphoreType.DMA((3,)),
            *landing,
        ],
        flops=width * width,
        moved=4 * width * width,
    )(*map(in_hbm, (amp_tile, task_rows, own, ints[0, 0])))
    slots = [own, *others]
    keep, give = call(pick_kernel, "pick", (tile, tile), [VMEM] * (1 + len(slots)))(facts, *slots)
    got = lax.ppermute(give, "dev", [(i, i ^ 1) for i in range(devs)])
    mine = call(merge_kernel, "merge", tile, [VMEM] * 3)(facts, keep, got)

    pieces = [mine] + [
        lax.ppermute(mine, "node", [(i, i ^ k) for i in range(nodes)])
        for k in range(1, nodes)
    ]
    denom, high_b, low_b = call(
        split_kernel,
        "split",
        (jax.ShapeDtypeStruct((nodes, groups, LANES), jnp.float32), half, half),
        [VMEM, pl.BlockSpec(memory_space=pltpu.SMEM), HBM, HBM],
        [pltpu.VMEM(virt_energy.shape, jnp.float32), pltpu.SemaphoreType.DMA, *landing],
        flops=width * width,
        moved=4 * width * width,
    )(mine, pair_energy, in_hbm(virt_energy), in_hbm(ints[0, 0]))
    products = call(
        product_kernel,
        "product",
        jax.ShapeDtypeStruct((nodes * pairs, groups, LANES), jnp.float32),
        [VMEM] * (5 + nodes),
        [pltpu.VMEM((nodes * pairs, width), jnp.float32)],
        flops=6 * nodes * pairs * width * width,
        moved=4 * width * width,
    )(facts, high_a, low_a, high_b, low_b, *pieces)

    terms = lax.all_to_all(products, ("node", "dev"), 0, 0, tiled=True)
    ladder = jnp.sum(terms.reshape(nodes, devs, groups, LANES), axis=1)
    return (ladder / denom).reshape(1, 1, nodes * width)


def solution(mesh):
    in_specs = (
        P("node", "dev", None, None),
        P(),
        P("node", "dev", None, None),
        P(),
        P("node", "dev"),
        P(),
    )
    return jax.shard_map(
        on_device, mesh=mesh, in_specs=in_specs, out_specs=P("node", "dev", None), check_vma=False
    )
```

time: 44.9 us -> 32 us (0.71)
  between operations: 8.32 us -> 0.73 us
  Pallas kernels: 0 us -> 5 us
  matrix products: 4.15 us -> 0 us
  waiting for transfers between devices: 7.59 us -> 5.11 us
  local copies, waits for them, and re-layouts: 2.11 us -> 0 us
  other arithmetic: 1.79 us -> 0.63 us
    all_to_all x0 -> x1, blocking collectives: none -> 11.4 us  [on_device(): terms = lax.all_to_all(products, ('node', 'dev'), 0, 0, tiled=True)]
    all_gather x1 -> x0, blocking collectives: 11.1 us -> none  [on_device(): slots = lax.all_gather(amps[0, 0], 'dev', axis=0)]
    all_to_all x1 -> x0, waiting for transfers between devices: 7.58 us -> none  [on_device(): terms = lax.all_to_all(products, ('node', 'dev'), 0, 0, tiled=True)]
    pallas_call x0 -> x5, Pallas kernels: none -> 5 us  [the longest x1 1.77 us: on_device(): call(stage_kernel, 'stage', (jax.ShapeDtypeStruct((HITS + nodes, LANES),...]
    all_to_all x1 -> x0, starting transfers between devices: 4.87 us -> none  [on_device(): terms = lax.all_to_all(products, ('node', 'dev'), 0, 0, tiled=True)]
    ppermute x0 -> x4, starting transfers between devices: none -> 4.53 us  [the longest x3 4.46 us: on_device(): lax.ppermute(own, 'dev', [(i, i ^ k) for i in range(devs)])]
    dot_general x1 -> x0, matrix products: 4.15 us -> none  [on_device(): lax.dot_general(ordered.reshape(nodes * pairs, width), ints[0, 0], (((1,)...]
    ppermute x0 -> x4, waiting for transfers between devices: none -> 3.47 us  [the longest x3 2.28 us: on_device(): lax.ppermute(own, 'dev', [(i, i ^ k) for i in range(devs)])]
  transfers between devices with their start and end apart: 4 -> 7, of which waited for: 1 -> 4; matrix products, arithmetic and copies ran while one was open for 4% -> 0% of each run, Pallas kernels for 0% -> 11%
where the time goes in v2:
time: 32 us; the launch traced here: 31.8 us
  blocking collectives  11.4 us (36%)
  starting transfers between devices  8.98 us (28%)
  waiting for transfers between devices  5.11 us (16%)
  Pallas kernels  5 us (16%)
  between operations  0.73 us (2%)
  other arithmetic  0.63 us (2%)
    all_to_all x1, blocking collectives, on_device(): terms = lax.all_to_all(products, ('node', 'dev'), 0, 0, tiled=True)  11.4 us
    ppermute x3, starting transfers between devices, on_device(): lax.ppermute(own, 'dev', [(i, i ^ k) for i in range(devs)])  4.46 us
    ppermute x3, starting transfers between devices, on_device(): lax.ppermute(mine, 'node', [(i, i ^ k) for i in range(nodes)])  4.45 us
    ppermute x3, waiting for transfers between devices, on_device(): lax.ppermute(own, 'dev', [(i, i ^ k) for i in range(devs)])  2.28 us
    pallas_call x1, Pallas kernels, on_device(): call(stage_kernel, 'stage', (jax.ShapeDtypeStruct((HITS + nodes, LANES),...  1.77 us
    pallas_call x1, Pallas kernels, on_device(): call(split_kernel, 'split', (jax.ShapeDtypeStruct((nodes, groups, LANES),...  1.73 us
    ppermute x3, waiting for transfers between devices, on_device(): lax.ppermute(mine, 'node', [(i, i ^ k) for i in range(nodes)])  1.64 us
    pallas_call x1, Pallas kernels, on_device(): call(product_kernel, 'product', jax.ShapeDtypeStruct((nodes * pairs, grou...  1.41 us
  transfers between devices with their start and end apart: 7, of which 4 were waited for; matrix products, arithmetic and copies ran while one was open for 0% of the time, Pallas kernels for 11%

profile of v2, /device:TPU:0, one launch (start us, length us, event | category | flops | bytes accessed | tf_op | source)
XLA Modules:
  0.0 31.8 jit_solution(8758974914852125191)
XLA Ops:
  0.0 3.9 %collective-permute-start.2 = (f32[8,1024]{1,0:T(8,128)}, f32[8,1024]{1,0:T(8,128)S(1)}, u32[]{:S(2)}, u32[]{:S(2)}) collective-permute-start(f32[8,1024]{1,0:T(8,128)} %bitcast.8), channel_id=1, source_target_pairs={{0,6},{1,7},{2,4},{3,5},{4,2},{5,3},{6,0},{7,1},{8,14},{9,15},{10,... | collective-permute-start | bytes 98312 | tf_op jit(solution)/shard_map/ppermute | solution.py:159
  3.9 0.5 %collective-permute-start.1 = (f32[8,1024]{1,0:T(8,128)}, f32[8,1024]{1,0:T(8,128)S(1)}, u32[]{:S(2)}, u32[]{:S(2)}) collective-permute-start(f32[8,1024]{1,0:T(8,128)} %bitcast.9), channel_id=1, source_target_pairs={{0,4},{1,5},{2,6},{3,7},{4,0},{5,1},{6,2},{7,3},{8,12},{9,13},{10,... | collective-permute-start | bytes 98312 | tf_op jit(solution)/shard_map/ppermute | solution.py:159
  4.4 0.1 collective-permute-start
  4.5 1.8 %stage.1 = (s32[6,128]{1,0:T(8,128)S(1)}, f32[8,1024]{1,0:T(8,128)S(1)}, bf16[512,1024]{1,0:T(8,128)(2,1)S(1)}, bf16[512,1024]{1,0:T(8,128)(2,1)S(1)}) custom-call(s32[4,8]{1,0:T(4,128)} %tile_hbm.1, s32[4,2,16]{2,1,0:T(2,128)} %bitcast.12, f32[8,1024]{1,0:T(8,128)} %bitcast.11, f32[1024,1024]{1,0:T(8,128)} %bitcast.6), custom_call_target="tpu_custom_call" | custom-call | flops 1048576 | bytes 4194304 | tf_op jit(solution)/shard_map/stage/pallas_call | solution.py:163
  6.2 0.0 collective-permute-done.2.refs_3_
  6.3 1.8 %collective-permute-done.1.refs_2_ = f32[8,1024]{1,0:T(8,128)S(1)} collective-permute-done((f32[8,1024]{1,0:T(8,128)}, f32[8,1024]{1,0:T(8,128)S(1)}, u32[]{:S(2)}, u32[]{:S(2)}) %collective-permute-start.1) | collective-permute-done | bytes 32800 | tf_op jit(solution)/shard_map/ppermute | solution.py:159
  8.0 0.5 %collective-permute-done.refs_1_ = f32[8,1024]{1,0:T(8,128)S(1)} collective-permute-done((f32[8,1024]{1,0:T(8,128)}, f32[8,1024]{1,0:T(8,128)S(1)}, u32[]{:S(2)}, u32[]{:S(2)}) %collective-permute-start) | collective-permute-done | bytes 32800 | tf_op jit(solution)/shard_map/ppermute | solution.py:159
  8.5 0.1 pick.1
  8.6 0.1 collective-permute-start.3
  8.7 1.2 %collective-permute-done.3.got_ref = f32[8,1024]{1,0:T(8,128)S(1)} collective-permute-done((f32[8,1024]{1,0:T(8,128)S(1)}, f32[8,1024]{1,0:T(8,128)S(1)}, u32[]{:S(2)}, u32[]{:S(2)}) %collective-permute-start.3) | collective-permute-done | bytes 32800 | tf_op jit(solution)/shard_map/ppermute | solution.py:184
  9.9 3.7 %collective-permute-start.6 = (f32[8,1024]{1,0:T(8,128)S(1)}, f32[8,1024]{1,0:T(8,128)S(1)}, u32[]{:S(2)}, u32[]{:S(2)}) collective-permute-start(f32[8,1024]{1,0:T(8,128)S(1)} %merge.1.after_ref.refs_0_), channel_id=1, source_target_pairs={{0,24},{8,16},{16,8},{24,0},{1,25},{9,17},{17,9},{25,1},{2,26},{10... | collective-permute-start | bytes 98312 | tf_op jit(solution)/shard_map/ppermute | solution.py:188
  13.6 0.0 collective-permute-start.5
  13.6 0.8 %collective-permute-start.4 = (f32[8,1024]{1,0:T(8,128)S(1)}, f32[8,1024]{1,0:T(8,128)S(1)}, u32[]{:S(2)}, u32[]{:S(2)}) collective-permute-start(f32[8,1024]{1,0:T(8,128)S(1)} %merge.1.after_ref.refs_0_), channel_id=1, source_target_pairs={{0,8},{8,0},{16,24},{24,16},{1,9},{9,1},{17,25},{25,17},{2,10},{10... | collective-permute-start | bytes 98312 | tf_op jit(solution)/shard_map/ppermute | solution.py:188
  15.0 1.7 %split.1 = (f32[4,8,128]{2,1,0:T(8,128)S(1)}, bf16[512,1024]{1,0:T(8,128)(2,1)S(1)}, bf16[512,1024]{1,0:T(8,128)(2,1)S(1)}) custom-call(f32[8,1024]{1,0:T(8,128)S(1)} %merge.1.after_ref.refs_0_, f32[1,1]{1,0:T(1,128)S(6)} %copy.7.pair_ref, f32[4,1024]{1,0:T(4,128)} %virt_hbm.1, f32[1024,1024]{1,0:T(8,128)} %bitcast.7), custom_call_target="tpu_custom_call" | custom-call | flops 1048576 | bytes 4194304 | tf_op jit(solution)/shard_map/split/pallas_call | solution.py:191
  16.8 0.0 collective-permute-done.6.refs_3_
  16.8 1.6 %collective-permute-done.5.refs_2_ = f32[8,1024]{1,0:T(8,128)S(1)} collective-permute-done((f32[8,1024]{1,0:T(8,128)S(1)}, f32[8,1024]{1,0:T(8,128)S(1)}, u32[]{:S(2)}, u32[]{:S(2)}) %collective-permute-start.5) | collective-permute-done | bytes 32800 | tf_op jit(solution)/shard_map/ppermute | solution.py:188
  18.4 0.0 collective-permute-done.4.refs_1_
  18.4 1.4 %product.1 = f32[32,8,128]{2,1,0:T(8,128)S(1)} custom-call(s32[6,128]{1,0:T(8,128)S(1)} %get-tuple-element.14.facts_ref, bf16[512,1024]{1,0:T(8,128)(2,1)S(1)} %get-tuple-element.15.high_a_ref, bf16[512,1024]{1,0:T(8,128)(2,1)S(1)} %get-tuple-element.16.low_a_ref, bf16[512,1024]{1,0:T(8,128)(2,1)S(1)} %get-tuple-element.20.high_b_ref, ...), custom_call_target="tpu_custom_call" | custom-call | flops 201326592 | bytes 4194304 | tf_op jit(solution)/shard_map/product/pallas_call | solution.py:200
  19.8 11.4 %all_to_all.5 = f32[32,8,128]{2,1,0:T(8,128)S(1)} all-to-all(f32[32,8,128]{2,1,0:T(8,128)S(1)} %product.1), channel_id=1, replica_groups=mesh['node'=4,'dev'=8] {'node','dev'}, dimensions={0} | all-to-all | bytes 262144 | tf_op jit(solution)/shard_map/all_to_all | solution.py:210
  31.2 0.6 %div.3 = f32[4,8,128]{2,1,0:T(8,128)} divide(f32[4,8,128]{2,1,0:T(8,128)S(1)} %bitcast_reduce_fusion, f32[4,8,128]{2,1,0:T(8,128)S(1)} %get-tuple-element.22) | non-fusion elementwise | flops 4096 | bytes 49152 | tf_op jit(solution)/shard_map/div | solution.py:212
  (2 shorter events, 0.1 us)
Async XLA Ops:
  0.0 6.2 %collective-permute-start.2 = (f32[8,1024]{1,0:T(8,128)}, f32[8,1024]{1,0:T(8,128)S(1)}, u32[]{:S(2)}, u32[]{:S(2)}) collective-permute-start(f32[8,1024]{1,0:T(8,128)} %bitcast.8), channel_id=1, source_target_pairs={{0,6},{1,7},{2,4},{3,5},{4,2},{5,3},{6,0},{7,1},{8,14},{9,15},{10,... | collective-permute-start | bytes 98312 | tf_op jit(solution)/shard_map/ppermute | solution.py:159
  3.9 4.1 %collective-permute-start.1 = (f32[8,1024]{1,0:T(8,128)}, f32[8,1024]{1,0:T(8,128)S(1)}, u32[]{:S(2)}, u32[]{:S(2)}) collective-permute-start(f32[8,1024]{1,0:T(8,128)} %bitcast.9), channel_id=1, source_target_pairs={{0,4},{1,5},{2,6},{3,7},{4,0},{5,1},{6,2},{7,3},{8,12},{9,13},{10,... | collective-permute-start | bytes 98312 | tf_op jit(solution)/shard_map/ppermute | solution.py:159
  4.4 4.1 %collective-permute-start = (f32[8,1024]{1,0:T(8,128)}, f32[8,1024]{1,0:T(8,128)S(1)}, u32[]{:S(2)}, u32[]{:S(2)}) collective-permute-start(f32[8,1024]{1,0:T(8,128)} %bitcast.10), channel_id=1, source_target_pairs={{0,2},{1,3},{2,0},{3,1},{4,6},{5,7},{6,4},{7,5},{8,10},{9,11},{10,... | collective-permute-start | bytes 98312 | tf_op jit(solution)/shard_map/ppermute | solution.py:159
  8.6 1.3 %collective-permute-start.3 = (f32[8,1024]{1,0:T(8,128)S(1)}, f32[8,1024]{1,0:T(8,128)S(1)}, u32[]{:S(2)}, u32[]{:S(2)}) collective-permute-start(f32[8,1024]{1,0:T(8,128)S(1)} %get-tuple-element.19), channel_id=1, source_target_pairs={{0,1},{1,0},{2,3},{3,2},{4,5},{5,4},{6,7},{7,6},{8,9},{9,8},{10,11... | collective-permute-start | bytes 98312 | tf_op jit(solution)/shard_map/ppermute | solution.py:184
  9.9 6.8 %collective-permute-start.6 = (f32[8,1024]{1,0:T(8,128)S(1)}, f32[8,1024]{1,0:T(8,128)S(1)}, u32[]{:S(2)}, u32[]{:S(2)}) collective-permute-start(f32[8,1024]{1,0:T(8,128)S(1)} %merge.1.after_ref.refs_0_), channel_id=1, source_target_pairs={{0,24},{8,16},{16,8},{24,0},{1,25},{9,17},{17,9},{25,1},{2,26},{10... | collective-permute-start | bytes 98312 | tf_op jit(solution)/shard_map/ppermute | solution.py:188
  13.6 4.8 %collective-permute-start.5 = (f32[8,1024]{1,0:T(8,128)S(1)}, f32[8,1024]{1,0:T(8,128)S(1)}, u32[]{:S(2)}, u32[]{:S(2)}) collective-permute-start(f32[8,1024]{1,0:T(8,128)S(1)} %merge.1.after_ref.refs_0_), channel_id=1, source_target_pairs={{0,16},{8,24},{16,0},{24,8},{1,17},{9,25},{17,1},{25,9},{2,18},{10... | collective-permute-start | bytes 98312 | tf_op jit(solution)/shard_map/ppermute | solution.py:188
  13.6 4.8 %collective-permute-start.4 = (f32[8,1024]{1,0:T(8,128)S(1)}, f32[8,1024]{1,0:T(8,128)S(1)}, u32[]{:S(2)}, u32[]{:S(2)}) collective-permute-start(f32[8,1024]{1,0:T(8,128)S(1)} %merge.1.after_ref.refs_0_), channel_id=1, source_target_pairs={{0,8},{8,0},{16,24},{24,16},{1,9},{9,1},{17,25},{25,17},{2,10},{10... | collective-permute-start | bytes 98312 | tf_op jit(solution)/shard_map/ppermute | solution.py:188

commit v3 on v2

v3 whole, which is shorter than its diff:
```python
import jax
import jax.numpy as jnp
from jax import lax
from jax.experimental import pallas as pl
from jax.experimental.pallas import tpu as pltpu
from jax.sharding import PartitionSpec as P

LANES = 128
VMEM_LIMIT = 24 * 2**20
CONTRACT_LAST = (((1,), (1,)), ((), ()))
HITS = 2
VMEM = pl.BlockSpec(memory_space=pltpu.VMEM)
HBM = pl.BlockSpec(memory_space=pltpu.HBM)
CHUNKS = 2


def call(kernel, name, out_shape, in_specs, scratch=(), flops=0, moved=0):
    return pl.pallas_call(
        kernel,
        out_shape=out_shape,
        in_specs=in_specs,
        out_specs=jax.tree.map(lambda _: VMEM, out_shape),
        scratch_shapes=list(scratch),
        compiler_params=pltpu.CompilerParams(vmem_limit_bytes=VMEM_LIMIT),
        cost_estimate=pl.CostEstimate(flops=flops, bytes_accessed=moved, transcendentals=0),
        name=name,
    )


def high_and_low(x):
    high = x.astype(jnp.bfloat16)
    return high, (x - high.astype(jnp.float32)).astype(jnp.bfloat16)


def split_rows(ints_hbm, first, land_ref, sems, high_ref, low_ref):
    chunks = sems.shape[0]
    rows = high_ref.shape[0] // chunks
    copies = [
        pltpu.make_async_copy(
            ints_hbm.at[pl.ds(first + i * rows, rows)], land_ref.at[pl.ds(i * rows, rows)], sems.at[i]
        )
        for i in range(chunks)
    ]
    for copy in copies:
        copy.start()

    def finish():
        for i, copy in enumerate(copies):
            copy.wait()
            part = pl.ds(i * rows, rows)
            high_ref[part, :], low_ref[part, :] = high_and_low(land_ref[part, :])

    return finish


def in_hbm(x):
    return pltpu.with_memory_space_constraint(x, pltpu.HBM)


def stage_kernel(
    pair_ref, tile_hbm, tasks_hbm, virt_hbm, amps_hbm, ints_hbm,
    facts_ref, denom_ref, own_ref, high_ref, low_ref,
    tile_ref, tasks_ref, virt_ref, sems, land_ref, ints_sems,
):
    copies = [
        pltpu.make_async_copy(src, dst, sems.at[i])
        for i, (src, dst) in enumerate(
            [
                (tile_hbm, tile_ref),
                (tasks_hbm, tasks_ref),
                (virt_hbm, virt_ref),
                (amps_hbm, own_ref),
            ]
        )
    ]
    for copy in copies:
        copy.start()
    finish = split_rows(ints_hbm, 0, land_ref, ints_sems, high_ref, low_ref)
    my_node, my_dev = lax.axis_index("node"), lax.axis_index("dev")
    nodes = tasks_ref.shape[0]
    for copy in copies:
        copy.wait()
    row = tile_ref[pl.ds(my_node, 1), :]
    position = lax.broadcasted_iota(jnp.int32, row.shape, 1)
    for core in range(2):
        owner = my_dev // 2 * 2 + core
        slot = jnp.sum(jnp.where(row == owner, position, 0), axis=1, keepdims=True)
        facts_ref[core : core + 1, :] = jnp.broadcast_to(slot, (1, LANES))
    for k in range(nodes):
        task = tasks_ref[my_node ^ k]
        hit = jnp.where((task[0:1] == my_node) & (task[1:2] == my_dev), 1, 0)
        hit = jnp.max(hit, axis=1, keepdims=True)
        facts_ref[HITS + k : HITS + k + 1, :] = jnp.broadcast_to(hit, (1, LANES))
    denom = pair_ref[0, 0] - virt_ref[...]
    for j in range(denom_ref.shape[1]):
        denom_ref[:, j, :] = denom[:, j * LANES : (j + 1) * LANES]
    finish()


def split_kernel(after_ref, ints_hbm, high_ref, low_ref, land_ref, sems):
    del after_ref
    split_rows(ints_hbm, ints_hbm.shape[0] - high_ref.shape[0], land_ref, sems, high_ref, low_ref)()


def pick_kernel(facts_ref, *refs):
    pieces, held_ref = refs[:-1], refs[-1]
    chip = lax.axis_index("dev") // 2
    for core in range(2):
        step = (facts_ref[core : core + 1, 0:1] // 2) ^ chip
        tile = pieces[0][...]
        for j, piece in enumerate(pieces[1:], 1):
            tile = jnp.where(step == j, piece[...], tile)
        held_ref[core] = tile


def merge_kernel(facts_ref, held_ref, got_ref, both_ref, mine_ref):
    my_core = lax.axis_index("dev") % 2
    for core in range(2):
        here = facts_ref[core : core + 1, 0:1] % 2 == my_core
        both_ref[core] = jnp.where(here, held_ref[core], got_ref[core])
    mine_ref[...] = both_ref[my_core]


def theirs_kernel(after_ref, both_ref, theirs_ref):
    del after_ref
    theirs_ref[...] = both_ref[1 - lax.axis_index("dev") % 2]


def product_kernel(facts_ref, high_a_ref, low_a_ref, high_b_ref, low_b_ref, mine_ref, last_ref, *refs):
    fetched, handed = refs[: len(refs) // 2 - 1], refs[len(refs) // 2 - 1 : -2]
    out_ref, rows_ref = refs[-2:]
    my_node, my_core = lax.axis_index("node"), lax.axis_index("dev") % 2
    pairs = mine_ref.shape[0]
    total = rows_ref.shape[0]

    def place(k, tile):
        start = pl.multiple_of((my_node ^ k) * pairs, pairs)
        hit = facts_ref[pl.ds(HITS + k, 1), 0:1]
        rows_ref[pl.ds(start, pairs), :] = jnp.where(hit > 0, tile, 0.0)

    place(0, mine_ref[...])
    place(2 * len(fetched) + 1, last_ref[...])
    for i, (fetched_ref, handed_ref) in enumerate(zip(fetched, handed)):
        place(2 * i + 1 + my_core, fetched_ref[my_core])
        place(2 * i + 2 - my_core, handed_ref[...])
    amp_high, amp_low = high_and_low(rows_ref[...])
    amps = jnp.concatenate([amp_high, amp_low], axis=0)
    first = 0
    for high_ref, low_ref in ((high_a_ref, low_a_ref), (high_b_ref, low_b_ref)):
        for j in range(high_ref.shape[0] // LANES):
            part = slice(j * LANES, (j + 1) * LANES)
            term = lax.dot_general(
                high_ref[part, :], amps, CONTRACT_LAST, preferred_element_type=jnp.float32
            ) + lax.dot_general(
                low_ref[part, :], amps, CONTRACT_LAST, preferred_element_type=jnp.float32
            )
            term = term.T
            out_ref[:, first + j, :] = term[:total] + term[total:]
        first += high_ref.shape[0] // LANES


def on_device(amps, amp_tile, ints, tasks, pair_energy, virt_energy):
    nodes, devs = lax.axis_size("node"), lax.axis_size("dev")
    pairs, width = amps.shape[2], amps.shape[3]
    groups = width // LANES
    tile = jax.ShapeDtypeStruct((pairs, width), jnp.float32)
    task_rows = jnp.swapaxes(tasks, 1, 2)

    own = amps[0, 0]
    others = [
        lax.ppermute(own, "dev", [(i, i ^ k) for i in range(devs)]) for k in range(2, devs, 2)
    ]
    half = jax.ShapeDtypeStruct((width // 2, width), jnp.bfloat16)
    landing = [pltpu.VMEM(half.shape, jnp.float32), pltpu.SemaphoreType.DMA((CHUNKS,))]
    facts, denom, own, high_a, low_a = call(
        stage_kernel,
        "stage",
        (
            jax.ShapeDtypeStruct((HITS + nodes, LANES), jnp.int32),
            jax.ShapeDtypeStruct((nodes, groups, LANES), jnp.float32),
            tile,
            half,
            half,
        ),
        [pl.BlockSpec(memory_space=pltpu.SMEM)] + [HBM] * 5,
        [
            pltpu.VMEM(amp_tile.shape, jnp.int32),
            pltpu.VMEM(task_rows.shape, jnp.int32),
            pltpu.VMEM(virt_energy.shape, jnp.float32),
            pltpu.SemaphoreType.DMA((4,)),
            *landing,
        ],
        flops=width * width,
        moved=4 * width * width,
    )(pair_energy, *map(in_hbm, (amp_tile, task_rows, virt_energy, own, ints[0, 0])))
    slots = [own, *others]
    both = jax.ShapeDtypeStruct((2, pairs, width), jnp.float32)
    swap = [(i, i ^ 1) for i in range(devs)]
    held = call(pick_kernel, "pick", both, [VMEM] * (1 + len(slots)))(facts, *slots)
    got = lax.ppermute(held, "dev", swap)
    chip_tiles, mine = call(merge_kernel, "merge", (both, tile), [VMEM] * 3)(facts, held, got)

    fetched = [
        lax.ppermute(
            chip_tiles,
            ("node", "dev"),
            [
                (n * devs + d, (n ^ (k + d % 2)) * devs + d)
                for n in range(nodes)
                for d in range(devs)
            ],
        )
        for k in range(1, nodes - 1, 2)
    ]
    last = lax.ppermute(mine, "node", [(i, i ^ (nodes - 1)) for i in range(nodes)])
    high_b, low_b = call(
        split_kernel,
        "split",
        (half, half),
        [VMEM, HBM],
        landing,
        flops=width * width,
        moved=4 * width * width,
    )(mine, in_hbm(ints[0, 0]))
    handed = [
        lax.ppermute(call(theirs_kernel, "theirs", tile, [VMEM] * 2)(high_b, tiles), "dev", swap)
        for tiles in fetched
    ]
    products = call(
        product_kernel,
        "product",
        jax.ShapeDtypeStruct((nodes * pairs, groups, LANES), jnp.float32),
        [VMEM] * (7 + 2 * len(fetched)),
        [pltpu.VMEM((nodes * pairs, width), jnp.float32)],
        flops=6 * nodes * pairs * width * width,
        moved=4 * width * width,
    )(facts, high_a, low_a, high_b, low_b, mine, last, *fetched, *handed)

    terms = lax.all_to_all(products, ("node", "dev"), 0, 0, tiled=True)
    ladder = jnp.sum(terms.reshape(nodes, devs, groups, LANES), axis=1)
    return (ladder / denom).reshape(1, 1, nodes * width)


def solution(mesh):
    in_specs = (
        P("node", "dev", None, None),
        P(),
        P("node", "dev", None, None),
        P(),
        P("node", "dev"),
        P(),
    )
    return jax.shard_map(
        on_device, mesh=mesh, in_specs=in_specs, out_specs=P("node", "dev", None), check_vma=False
    )
```

time: 32 us -> 31.5 us (0.984)
  waiting for transfers between devices: 5.11 us -> 4.53 us
    ppermute x3, waiting for transfers between devices: 2.28 us -> 1.6 us  [on_device(): lax.ppermute(own, 'dev', [(i, i ^ k) for i in range(devs)])]
    pallas_call x3 -> x4, Pallas kernels: 1.83 us -> 1.82 us  [the longest x1 1.7 us: on_device(): call(split_kernel, 'split', (half, half), [VMEM, HBM], landing, flops=wid...]
where the time goes in v3:
time: 31.5 us; the launch traced here: 31.3 us
  blocking collectives  11.7 us (37%)
  starting transfers between devices  8.72 us (28%)
  Pallas kernels  4.98 us (16%)
  waiting for transfers between devices  4.53 us (14%)
  between operations  0.74 us (2%)
  other arithmetic  0.63 us (2%)
    all_to_all x1, blocking collectives, on_device(): terms = lax.all_to_all(products, ('node', 'dev'), 0, 0, tiled=True)  11.7 us
    ppermute x3, starting transfers between devices, on_device(): lax.ppermute(own, 'dev', [(i, i ^ k) for i in range(devs)])  4.46 us
    ppermute x1, starting transfers between devices, on_device(): lax.ppermute(mine, 'node', [(i, i ^ nodes - 1) for i in range(nodes)])  2.47 us
    pallas_call x1, Pallas kernels, on_device(): call(stage_kernel, 'stage', (jax.ShapeDtypeStruct((HITS + nodes, LANES),...  1.8 us
    pallas_call x1, Pallas kernels, on_device(): call(split_kernel, 'split', (half, half), [VMEM, HBM], landing, flops=wid...  1.7 us
    ppermute x1, waiting for transfers between devices, on_device(): lax.ppermute(mine, 'node', [(i, i ^ nodes - 1) for i in range(nodes)])  1.69 us
    ppermute x1, starting transfers between devices, on_device(): lax.ppermute(chip_tiles, ('node', 'dev'), [(n * devs + d, (n ^ k + d % 2)...  1.64 us
    ppermute x3, waiting for transfers between devices, on_device(): lax.ppermute(own, 'dev', [(i, i ^ k) for i in range(devs)])  1.6 us
  transfers between devices with their start and end apart: 7, of which 4 were waited for; matrix products, arithmetic and copies ran while one was open for 0% of the time, Pallas kernels for 11%

profile of v3, /device:TPU:0, one launch (start us, length us, event | category | flops | bytes accessed | tf_op | source)
XLA Modules:
  0.0 31.3 jit_solution(15997737486889530069)
XLA Ops:
  0.0 3.9 %collective-permute-start.2 = (f32[8,1024]{1,0:T(8,128)}, f32[8,1024]{1,0:T(8,128)S(1)}, u32[]{:S(2)}, u32[]{:S(2)}) collective-permute-start(f32[8,1024]{1,0:T(8,128)} %bitcast.8), channel_id=1, source_target_pairs={{0,6},{1,7},{2,4},{3,5},{4,2},{5,3},{6,0},{7,1},{8,14},{9,15},{10,... | collective-permute-start | bytes 98312 | tf_op jit(solution)/shard_map/ppermute | solution.py:171
  3.9 0.5 %collective-permute-start.1 = (f32[8,1024]{1,0:T(8,128)}, f32[8,1024]{1,0:T(8,128)S(1)}, u32[]{:S(2)}, u32[]{:S(2)}) collective-permute-start(f32[8,1024]{1,0:T(8,128)} %bitcast.9), channel_id=1, source_target_pairs={{0,4},{1,5},{2,6},{3,7},{4,0},{5,1},{6,2},{7,3},{8,12},{9,13},{10,... | collective-permute-start | bytes 98312 | tf_op jit(solution)/shard_map/ppermute | solution.py:171
  4.4 0.1 collective-permute-start
  5.1 1.8 %stage.1 = (s32[6,128]{1,0:T(8,128)S(1)}, f32[4,8,128]{2,1,0:T(8,128)S(1)}, f32[8,1024]{1,0:T(8,128)S(1)}, bf16[512,1024]{1,0:T(8,128)(2,1)S(1)}, bf16[512,1024]{1,0:T(8,128)(2,1)S(1)}) custom-call(f32[1,1]{1,0:T(1,128)S(6)} %copy.7.pair_ref, s32[4,8]{1,0:T(4,128)} %tile_hbm.1, s32[4,2,16]{2,1,0:T(2,128)} %bitcast.12, f32[4,1024]{1,0:T(4,128)} %virt_hbm.1, ...), custom_call_target="tpu_custom_call" | custom-call | flops 1048576 | bytes 4194304 | tf_op jit(solution)/shard_map/stage/pallas_call | solution.py:175
  6.9 0.0 collective-permute-done.2.refs_3_
  6.9 1.1 %collective-permute-done.1.refs_2_ = f32[8,1024]{1,0:T(8,128)S(1)} collective-permute-done((f32[8,1024]{1,0:T(8,128)}, f32[8,1024]{1,0:T(8,128)S(1)}, u32[]{:S(2)}, u32[]{:S(2)}) %collective-permute-start.1) | collective-permute-done | bytes 32800 | tf_op jit(solution)/shard_map/ppermute | solution.py:171
  8.0 0.5 %collective-permute-done.refs_1_ = f32[8,1024]{1,0:T(8,128)S(1)} collective-permute-done((f32[8,1024]{1,0:T(8,128)}, f32[8,1024]{1,0:T(8,128)S(1)}, u32[]{:S(2)}, u32[]{:S(2)}) %collective-permute-start) | collective-permute-done | bytes 32800 | tf_op jit(solution)/shard_map/ppermute | solution.py:171
  8.5 0.1 pick.1.held_ref
  8.6 0.1 collective-permute-start.3
  8.7 1.2 %collective-permute-done.3.got_ref = f32[2,8,1024]{2,1,0:T(8,128)S(1)} collective-permute-done((f32[2,8,1024]{2,1,0:T(8,128)S(1)}, f32[2,8,1024]{2,1,0:T(8,128)S(1)}, u32[]{:S(2)}, u32[]{:S(2)}) %collective-permute-start.3) | collective-permute-done | bytes 65568 | tf_op jit(solution)/shard_map/ppermute | solution.py:200
  9.9 0.1 merge.1
  10.0 1.6 %collective-permute-start.5 = (f32[2,8,1024]{2,1,0:T(8,128)S(1)}, f32[2,8,1024]{2,1,0:T(8,128)S(1)}, u32[]{:S(2)}, u32[]{:S(2)}) collective-permute-start(f32[2,8,1024]{2,1,0:T(8,128)S(1)} %get-tuple-element.21), channel_id=1, source_target_pairs={{0,8},{1,17},{2,10},{3,19},{4,12},{5,21},{6,14},{7,23},{8,0},{9,25... | collective-permute-start | bytes 196616 | tf_op jit(solution)/shard_map/ppermute | solution.py:204
  11.6 2.5 %collective-permute-start.4 = (f32[8,1024]{1,0:T(8,128)S(1)}, f32[8,1024]{1,0:T(8,128)S(1)}, u32[]{:S(2)}, u32[]{:S(2)}) collective-permute-start(f32[8,1024]{1,0:T(8,128)S(1)} %get-tuple-element.18.after_ref.mine_ref), channel_id=1, source_target_pairs={{0,24},{8,16},{16,8},{24,0},{1,25},{9,17},{17,9},{25,1},{2,26},{10... | collective-permute-start | bytes 98312 | tf_op jit(solution)/shard_map/ppermute | solution.py:215
  14.1 1.7 %split.1 = (bf16[512,1024]{1,0:T(8,128)(2,1)S(1)}, bf16[512,1024]{1,0:T(8,128)(2,1)S(1)}) custom-call(f32[8,1024]{1,0:T(8,128)S(1)} %get-tuple-element.18.after_ref.mine_ref, f32[1024,1024]{1,0:T(8,128)} %bitcast.7), custom_call_target="tpu_custom_call" | custom-call | flops 1048576 | bytes 4194304 | tf_op jit(solution)/shard_map/split/pallas_call | solution.py:216
  15.8 0.0 collective-permute-done.5.both_ref.refs_0_
  15.8 0.1 collective-permute-start.6
  15.9 1.7 %collective-permute-done.4.last_ref = f32[8,1024]{1,0:T(8,128)S(1)} collective-permute-done((f32[8,1024]{1,0:T(8,128)S(1)}, f32[8,1024]{1,0:T(8,128)S(1)}, u32[]{:S(2)}, u32[]{:S(2)}) %collective-permute-start.4) | collective-permute-done | bytes 32800 | tf_op jit(solution)/shard_map/ppermute | solution.py:215
  17.6 0.0 collective-permute-done.6.refs_1_
  17.6 1.4 %product.1 = f32[32,8,128]{2,1,0:T(8,128)S(1)} custom-call(s32[6,128]{1,0:T(8,128)S(1)} %get-tuple-element.14.facts_ref, bf16[512,1024]{1,0:T(8,128)(2,1)S(1)} %get-tuple-element.15.high_a_ref, bf16[512,1024]{1,0:T(8,128)(2,1)S(1)} %get-tuple-element.16.low_a_ref, bf16[512,1024]{1,0:T(8,128)(2,1)S(1)} %get-tuple-element.19.after_ref.high_b_ref, ...), custom_call_target="tpu_custom_call" | custom-call | flops 201326592 | bytes 4194304 | tf_op jit(solution)/shard_map/product/pallas_call | solution.py:229
  19.0 11.7 %all_to_all.5 = f32[32,8,128]{2,1,0:T(8,128)S(1)} all-to-all(f32[32,8,128]{2,1,0:T(8,128)S(1)} %product.1), channel_id=1, replica_groups=mesh['node'=4,'dev'=8] {'node','dev'}, dimensions={0} | all-to-all | bytes 262144 | tf_op jit(solution)/shard_map/all_to_all | solution.py:239
  30.7 0.6 %div.3 = f32[4,8,128]{2,1,0:T(8,128)} divide(f32[4,8,128]{2,1,0:T(8,128)S(1)} %bitcast_reduce_fusion, f32[4,8,128]{2,1,0:T(8,128)S(1)} %get-tuple-element.22) | non-fusion elementwise | flops 4096 | bytes 49152 | tf_op jit(solution)/shard_map/div | solution.py:241
  (2 shorter events, 0.0 us)
Async XLA Ops:
  0.0 6.9 %collective-permute-start.2 = (f32[8,1024]{1,0:T(8,128)}, f32[8,1024]{1,0:T(8,128)S(1)}, u32[]{:S(2)}, u32[]{:S(2)}) collective-permute-start(f32[8,1024]{1,0:T(8,128)} %bitcast.8), channel_id=1, source_target_pairs={{0,6},{1,7},{2,4},{3,5},{4,2},{5,3},{6,0},{7,1},{8,14},{9,15},{10,... | collective-permute-start | bytes 98312 | tf_op jit(solution)/shard_map/ppermute | solution.py:171
  3.9 4.1 %collective-permute-start.1 = (f32[8,1024]{1,0:T(8,128)}, f32[8,1024]{1,0:T(8,128)S(1)}, u32[]{:S(2)}, u32[]{:S(2)}) collective-permute-start(f32[8,1024]{1,0:T(8,128)} %bitcast.9), channel_id=1, source_target_pairs={{0,4},{1,5},{2,6},{3,7},{4,0},{5,1},{6,2},{7,3},{8,12},{9,13},{10,... | collective-permute-start | bytes 98312 | tf_op jit(solution)/shard_map/ppermute | solution.py:171
  4.4 4.1 %collective-permute-start = (f32[8,1024]{1,0:T(8,128)}, f32[8,1024]{1,0:T(8,128)S(1)}, u32[]{:S(2)}, u32[]{:S(2)}) collective-permute-start(f32[8,1024]{1,0:T(8,128)} %bitcast.10), channel_id=1, source_target_pairs={{0,2},{1,3},{2,0},{3,1},{4,6},{5,7},{6,4},{7,5},{8,10},{9,11},{10,... | collective-permute-start | bytes 98312 | tf_op jit(solution)/shard_map/ppermute | solution.py:171
  8.6 1.3 %collective-permute-start.3 = (f32[2,8,1024]{2,1,0:T(8,128)S(1)}, f32[2,8,1024]{2,1,0:T(8,128)S(1)}, u32[]{:S(2)}, u32[]{:S(2)}) collective-permute-start(f32[2,8,1024]{2,1,0:T(8,128)S(1)} %pick.1.held_ref), channel_id=1, source_target_pairs={{0,1},{1,0},{2,3},{3,2},{4,5},{5,4},{6,7},{7,6},{8,9},{9,8},{10,11... | collective-permute-start | bytes 196616 | tf_op jit(solution)/shard_map/ppermute | solution.py:200
  10.0 5.8 %collective-permute-start.5 = (f32[2,8,1024]{2,1,0:T(8,128)S(1)}, f32[2,8,1024]{2,1,0:T(8,128)S(1)}, u32[]{:S(2)}, u32[]{:S(2)}) collective-permute-start(f32[2,8,1024]{2,1,0:T(8,128)S(1)} %get-tuple-element.21), channel_id=1, source_target_pairs={{0,8},{1,17},{2,10},{3,19},{4,12},{5,21},{6,14},{7,23},{8,0},{9,25... | collective-permute-start | bytes 196616 | tf_op jit(solution)/shard_map/ppermute | solution.py:204
  11.6 6.0 %collective-permute-start.4 = (f32[8,1024]{1,0:T(8,128)S(1)}, f32[8,1024]{1,0:T(8,128)S(1)}, u32[]{:S(2)}, u32[]{:S(2)}) collective-permute-start(f32[8,1024]{1,0:T(8,128)S(1)} %get-tuple-element.18.after_ref.mine_ref), channel_id=1, source_target_pairs={{0,24},{8,16},{16,8},{24,0},{1,25},{9,17},{17,9},{25,1},{2,26},{10... | collective-permute-start | bytes 98312 | tf_op jit(solution)/shard_map/ppermute | solution.py:215
  15.8 1.8 %collective-permute-start.6 = (f32[8,1024]{1,0:T(8,128)S(1)}, f32[8,1024]{1,0:T(8,128)S(1)}, u32[]{:S(2)}, u32[]{:S(2)}) collective-permute-start(f32[8,1024]{1,0:T(8,128)S(1)} %theirs.1), channel_id=1, source_target_pairs={{0,1},{1,0},{2,3},{3,2},{4,5},{5,4},{6,7},{7,6},{8,9},{9,8},{10,11... | collective-permute-start | bytes 98312 | tf_op jit(solution)/shard_map/ppermute | solution.py:226

commit v4 on v3

--- a/solution.py
+++ b/solution.py
@@ -7,7 +7,6 @@
 
 LANES = 128
 VMEM_LIMIT = 24 * 2**20
-CONTRACT_LAST = (((1,), (1,)), ((), ()))
 HITS = 2
 VMEM = pl.BlockSpec(memory_space=pltpu.VMEM)
 HBM = pl.BlockSpec(memory_space=pltpu.HBM)
@@ -34,7 +33,7 @@
 
 def split_rows(ints_hbm, first, land_ref, sems, high_ref, low_ref):
     chunks = sems.shape[0]
-    rows = high_ref.shape[0] // chunks
+    rows = high_ref.shape[1] // chunks
     copies = [
         pltpu.make_async_copy(
             ints_hbm.at[pl.ds(first + i * rows, rows)], land_ref.at[pl.ds(i * rows, rows)], sems.at[i]
@@ -47,8 +46,8 @@
     def finish():
         for i, copy in enumerate(copies):
             copy.wait()
-            part = pl.ds(i * rows, rows)
-            high_ref[part, :], low_ref[part, :] = high_and_low(land_ref[part, :])
+            part = slice(i * rows, (i + 1) * rows)
+            high_ref[:, part], low_ref[:, part] = high_and_low(land_ref[part, :].T)
 
     return finish
 
@@ -99,7 +98,7 @@
 
 def split_kernel(after_ref, ints_hbm, high_ref, low_ref, land_ref, sems):
     del after_ref
-    split_rows(ints_hbm, ints_hbm.shape[0] - high_ref.shape[0], land_ref, sems, high_ref, low_ref)()
+    split_rows(ints_hbm, ints_hbm.shape[0] - high_ref.shape[1], land_ref, sems, high_ref, low_ref)()
 
 
 def pick_kernel(facts_ref, *refs):
@@ -144,19 +143,15 @@
         place(2 * i + 1 + my_core, fetched_ref[my_core])
         place(2 * i + 2 - my_core, handed_ref[...])
     amp_high, amp_low = high_and_low(rows_ref[...])
-    amps = jnp.concatenate([amp_high, amp_low], axis=0)
+    amp_both = jnp.concatenate([amp_high, amp_low], axis=0)
     first = 0
     for high_ref, low_ref in ((high_a_ref, low_a_ref), (high_b_ref, low_b_ref)):
-        for j in range(high_ref.shape[0] // LANES):
-            part = slice(j * LANES, (j + 1) * LANES)
-            term = lax.dot_general(
-                high_ref[part, :], amps, CONTRACT_LAST, preferred_element_type=jnp.float32
-            ) + lax.dot_general(
-                low_ref[part, :], amps, CONTRACT_LAST, preferred_element_type=jnp.float32
-            )
-            term = term.T
-            out_ref[:, first + j, :] = term[:total] + term[total:]
-        first += high_ref.shape[0] // LANES
+        both = jnp.dot(amp_both, high_ref[...], preferred_element_type=jnp.float32)
+        rest = jnp.dot(amp_high, low_ref[...], preferred_element_type=jnp.float32)
+        result = both[:total] + (both[total:] + rest)
+        for j in range(high_ref.shape[1] // LANES):
+            out_ref[:, first + j, :] = result[:, j * LANES : (j + 1) * LANES]
+        first += high_ref.shape[1] // LANES
 
 
 def on_device(amps, amp_tile, ints, tasks, pair_energy, virt_energy):
@@ -170,8 +165,8 @@
     others = [
         lax.ppermute(own, "dev", [(i, i ^ k) for i in range(devs)]) for k in range(2, devs, 2)
     ]
-    half = jax.ShapeDtypeStruct((width // 2, width), jnp.bfloat16)
-    landing = [pltpu.VMEM(half.shape, jnp.float32), pltpu.SemaphoreType.DMA((CHUNKS,))]
+    half = jax.ShapeDtypeStruct((width, width // 2), jnp.bfloat16)
+    landing = [pltpu.VMEM((width // 2, width), jnp.float32), pltpu.SemaphoreType.DMA((CHUNKS,))]
     facts, denom, own, high_a, low_a = call(
         stage_kernel,
         "stage",

time: 31.5 us -> 31.1 us (0.987)
  waiting for transfers between devices: 4.53 us -> 4.08 us
    pallas_call x1, Pallas kernels: 1.36 us -> 0.9 us  [on_device(): call(product_kernel, 'product', jax.ShapeDtypeStruct((nodes * pairs, grou...]
  transfers between devices with their start and end apart: 7 -> 7, of which waited for: 4 -> 4; matrix products, arithmetic and copies ran while one was open for 0% -> 0% of each run, Pallas kernels for 11% -> 13%
where the time goes in v4:
time: 31.1 us; the launch traced here: 30.9 us
  blocking collectives  11.7 us (38%)
  starting transfers between devices  8.72 us (28%)
  Pallas kernels  4.98 us (16%)
  waiting for transfers between devices  4.08 us (13%)
  between operations  0.74 us (2%)
  other arithmetic  0.63 us (2%)
    all_to_all x1, blocking collectives, on_device(): terms = lax.all_to_all(products, ('node', 'dev'), 0, 0, tiled=True)  11.7 us
    ppermute x3, starting transfers between devices, on_device(): lax.ppermute(own, 'dev', [(i, i ^ k) for i in range(devs)])  4.46 us
    ppermute x1, starting transfers between devices, on_device(): lax.ppermute(mine, 'node', [(i, i ^ nodes - 1) for i in range(nodes)])  2.47 us
    pallas_call x1, Pallas kernels, on_device(): call(stage_kernel, 'stage', (jax.ShapeDtypeStruct((HITS + nodes, LANES),...  2.03 us
    pallas_call x1, Pallas kernels, on_device(): call(split_kernel, 'split', (half, half), [VMEM, HBM], landing, flops=wid...  1.92 us
    ppermute x1, starting transfers between devices, on_device(): lax.ppermute(chip_tiles, ('node', 'dev'), [(n * devs + d, (n ^ k + d % 2)...  1.64 us
    ppermute x1, waiting for transfers between devices, on_device(): lax.ppermute(mine, 'node', [(i, i ^ nodes - 1) for i in range(nodes)])  1.46 us
    ppermute x3, waiting for transfers between devices, on_device(): lax.ppermute(own, 'dev', [(i, i ^ k) for i in range(devs)])  1.37 us
  transfers between devices with their start and end apart: 7, of which 4 were waited for; matrix products, arithmetic and copies ran while one was open for 0% of the time, Pallas kernels for 13%

profile of v4, /device:TPU:0, one launch (start us, length us, event | category | flops | bytes accessed | tf_op | source)
XLA Modules:
  0.0 30.9 jit_solution(14072663075783366174)
XLA Ops:
  0.0 3.9 %collective-permute-start.2 = (f32[8,1024]{1,0:T(8,128)}, f32[8,1024]{1,0:T(8,128)S(1)}, u32[]{:S(2)}, u32[]{:S(2)}) collective-permute-start(f32[8,1024]{1,0:T(8,128)} %bitcast.8), channel_id=1, source_target_pairs={{0,6},{1,7},{2,4},{3,5},{4,2},{5,3},{6,0},{7,1},{8,14},{9,15},{10,... | collective-permute-start | bytes 98312 | tf_op jit(solution)/shard_map/ppermute | solution.py:166
  3.9 0.5 %collective-permute-start.1 = (f32[8,1024]{1,0:T(8,128)}, f32[8,1024]{1,0:T(8,128)S(1)}, u32[]{:S(2)}, u32[]{:S(2)}) collective-permute-start(f32[8,1024]{1,0:T(8,128)} %bitcast.9), channel_id=1, source_target_pairs={{0,4},{1,5},{2,6},{3,7},{4,0},{5,1},{6,2},{7,3},{8,12},{9,13},{10,... | collective-permute-start | bytes 98312 | tf_op jit(solution)/shard_map/ppermute | solution.py:166
  4.4 0.1 collective-permute-start
  5.1 2.0 %stage.1 = (s32[6,128]{1,0:T(8,128)S(1)}, f32[4,8,128]{2,1,0:T(8,128)S(1)}, f32[8,1024]{1,0:T(8,128)S(1)}, bf16[1024,512]{1,0:T(8,128)(2,1)S(1)}, bf16[1024,512]{1,0:T(8,128)(2,1)S(1)}) custom-call(f32[1,1]{1,0:T(1,128)S(6)} %copy.7.pair_ref, s32[4,8]{1,0:T(4,128)} %tile_hbm.1, s32[4,2,16]{2,1,0:T(2,128)} %bitcast.12, f32[4,1024]{1,0:T(4,128)} %virt_hbm.1, ...), custom_call_target="tpu_custom_call" | custom-call | flops 1048576 | bytes 4194304 | tf_op jit(solution)/shard_map/stage/pallas_call | solution.py:170
  7.1 0.0 collective-permute-done.2.refs_3_
  7.2 0.9 %collective-permute-done.1.refs_2_ = f32[8,1024]{1,0:T(8,128)S(1)} collective-permute-done((f32[8,1024]{1,0:T(8,128)}, f32[8,1024]{1,0:T(8,128)S(1)}, u32[]{:S(2)}, u32[]{:S(2)}) %collective-permute-start.1) | collective-permute-done | bytes 32800 | tf_op jit(solution)/shard_map/ppermute | solution.py:166
  8.0 0.5 %collective-permute-done.refs_1_ = f32[8,1024]{1,0:T(8,128)S(1)} collective-permute-done((f32[8,1024]{1,0:T(8,128)}, f32[8,1024]{1,0:T(8,128)S(1)}, u32[]{:S(2)}, u32[]{:S(2)}) %collective-permute-start) | collective-permute-done | bytes 32800 | tf_op jit(solution)/shard_map/ppermute | solution.py:166
  8.5 0.1 pick.1.held_ref
  8.6 0.1 collective-permute-start.3
  8.7 1.2 %collective-permute-done.3.got_ref = f32[2,8,1024]{2,1,0:T(8,128)S(1)} collective-permute-done((f32[2,8,1024]{2,1,0:T(8,128)S(1)}, f32[2,8,1024]{2,1,0:T(8,128)S(1)}, u32[]{:S(2)}, u32[]{:S(2)}) %collective-permute-start.3) | collective-permute-done | bytes 65568 | tf_op jit(solution)/shard_map/ppermute | solution.py:195
  9.9 0.1 merge.1
  10.0 1.6 %collective-permute-start.5 = (f32[2,8,1024]{2,1,0:T(8,128)S(1)}, f32[2,8,1024]{2,1,0:T(8,128)S(1)}, u32[]{:S(2)}, u32[]{:S(2)}) collective-permute-start(f32[2,8,1024]{2,1,0:T(8,128)S(1)} %get-tuple-element.21), channel_id=1, source_target_pairs={{0,8},{1,17},{2,10},{3,19},{4,12},{5,21},{6,14},{7,23},{8,0},{9,25... | collective-permute-start | bytes 196616 | tf_op jit(solution)/shard_map/ppermute | solution.py:199
  11.6 2.5 %collective-permute-start.4 = (f32[8,1024]{1,0:T(8,128)S(1)}, f32[8,1024]{1,0:T(8,128)S(1)}, u32[]{:S(2)}, u32[]{:S(2)}) collective-permute-start(f32[8,1024]{1,0:T(8,128)S(1)} %get-tuple-element.18.after_ref.mine_ref), channel_id=1, source_target_pairs={{0,24},{8,16},{16,8},{24,0},{1,25},{9,17},{17,9},{25,1},{2,26},{10... | collective-permute-start | bytes 98312 | tf_op jit(solution)/shard_map/ppermute | solution.py:210
  14.1 1.9 %split.1 = (bf16[1024,512]{1,0:T(8,128)(2,1)S(1)}, bf16[1024,512]{1,0:T(8,128)(2,1)S(1)}) custom-call(f32[8,1024]{1,0:T(8,128)S(1)} %get-tuple-element.18.after_ref.mine_ref, f32[1024,1024]{1,0:T(8,128)} %bitcast.7), custom_call_target="tpu_custom_call" | custom-call | flops 1048576 | bytes 4194304 | tf_op jit(solution)/shard_map/split/pallas_call | solution.py:211
  16.0 0.0 collective-permute-done.5.both_ref.refs_0_
  16.1 0.1 collective-permute-start.6
  16.1 1.5 %collective-permute-done.4.last_ref = f32[8,1024]{1,0:T(8,128)S(1)} collective-permute-done((f32[8,1024]{1,0:T(8,128)S(1)}, f32[8,1024]{1,0:T(8,128)S(1)}, u32[]{:S(2)}, u32[]{:S(2)}) %collective-permute-start.4) | collective-permute-done | bytes 32800 | tf_op jit(solution)/shard_map/ppermute | solution.py:210
  17.6 0.0 collective-permute-done.6.refs_1_
  17.6 0.9 %product.1 = f32[32,8,128]{2,1,0:T(8,128)S(1)} custom-call(s32[6,128]{1,0:T(8,128)S(1)} %get-tuple-element.14.facts_ref, bf16[1024,512]{1,0:T(8,128)(2,1)S(1)} %get-tuple-element.15.high_a_ref, bf16[1024,512]{1,0:T(8,128)(2,1)S(1)} %get-tuple-element.16.low_a_ref, bf16[1024,512]{1,0:T(8,128)(2,1)S(1)} %get-tuple-element.19.after_ref.high_b_ref, ...), custom_call_target="tpu_custom_call" | custom-call | flops 201326592 | bytes 4194304 | tf_op jit(solution)/shard_map/product/pallas_call | solution.py:224
  18.5 11.7 %all_to_all.5 = f32[32,8,128]{2,1,0:T(8,128)S(1)} all-to-all(f32[32,8,128]{2,1,0:T(8,128)S(1)} %product.1), channel_id=1, replica_groups=mesh['node'=4,'dev'=8] {'node','dev'}, dimensions={0} | all-to-all | bytes 262144 | tf_op jit(solution)/shard_map/all_to_all | solution.py:234
  30.3 0.6 %div.3 = f32[4,8,128]{2,1,0:T(8,128)} divide(f32[4,8,128]{2,1,0:T(8,128)S(1)} %bitcast_reduce_fusion, f32[4,8,128]{2,1,0:T(8,128)S(1)} %get-tuple-element.22) | non-fusion elementwise | flops 4096 | bytes 49152 | tf_op jit(solution)/shard_map/div | solution.py:236
  (2 shorter events, 0.0 us)
Async XLA Ops:
  0.0 7.2 %collective-permute-start.2 = (f32[8,1024]{1,0:T(8,128)}, f32[8,1024]{1,0:T(8,128)S(1)}, u32[]{:S(2)}, u32[]{:S(2)}) collective-permute-start(f32[8,1024]{1,0:T(8,128)} %bitcast.8), channel_id=1, source_target_pairs={{0,6},{1,7},{2,4},{3,5},{4,2},{5,3},{6,0},{7,1},{8,14},{9,15},{10,... | collective-permute-start | bytes 98312 | tf_op jit(solution)/shard_map/ppermute | solution.py:166
  3.9 4.1 %collective-permute-start.1 = (f32[8,1024]{1,0:T(8,128)}, f32[8,1024]{1,0:T(8,128)S(1)}, u32[]{:S(2)}, u32[]{:S(2)}) collective-permute-start(f32[8,1024]{1,0:T(8,128)} %bitcast.9), channel_id=1, source_target_pairs={{0,4},{1,5},{2,6},{3,7},{4,0},{5,1},{6,2},{7,3},{8,12},{9,13},{10,... | collective-permute-start | bytes 98312 | tf_op jit(solution)/shard_map/ppermute | solution.py:166
  4.4 4.1 %collective-permute-start = (f32[8,1024]{1,0:T(8,128)}, f32[8,1024]{1,0:T(8,128)S(1)}, u32[]{:S(2)}, u32[]{:S(2)}) collective-permute-start(f32[8,1024]{1,0:T(8,128)} %bitcast.10), channel_id=1, source_target_pairs={{0,2},{1,3},{2,0},{3,1},{4,6},{5,7},{6,4},{7,5},{8,10},{9,11},{10,... | collective-permute-start | bytes 98312 | tf_op jit(solution)/shard_map/ppermute | solution.py:166
  8.6 1.3 %collective-permute-start.3 = (f32[2,8,1024]{2,1,0:T(8,128)S(1)}, f32[2,8,1024]{2,1,0:T(8,128)S(1)}, u32[]{:S(2)}, u32[]{:S(2)}) collective-permute-start(f32[2,8,1024]{2,1,0:T(8,128)S(1)} %pick.1.held_ref), channel_id=1, source_target_pairs={{0,1},{1,0},{2,3},{3,2},{4,5},{5,4},{6,7},{7,6},{8,9},{9,8},{10,11... | collective-permute-start | bytes 196616 | tf_op jit(solution)/shard_map/ppermute | solution.py:195
  10.0 6.1 %collective-permute-start.5 = (f32[2,8,1024]{2,1,0:T(8,128)S(1)}, f32[2,8,1024]{2,1,0:T(8,128)S(1)}, u32[]{:S(2)}, u32[]{:S(2)}) collective-permute-start(f32[2,8,1024]{2,1,0:T(8,128)S(1)} %get-tuple-element.21), channel_id=1, source_target_pairs={{0,8},{1,17},{2,10},{3,19},{4,12},{5,21},{6,14},{7,23},{8,0},{9,25... | collective-permute-start | bytes 196616 | tf_op jit(solution)/shard_map/ppermute | solution.py:199
  11.6 6.0 %collective-permute-start.4 = (f32[8,1024]{1,0:T(8,128)S(1)}, f32[8,1024]{1,0:T(8,128)S(1)}, u32[]{:S(2)}, u32[]{:S(2)}) collective-permute-start(f32[8,1024]{1,0:T(8,128)S(1)} %get-tuple-element.18.after_ref.mine_ref), channel_id=1, source_target_pairs={{0,24},{8,16},{16,8},{24,0},{1,25},{9,17},{17,9},{25,1},{2,26},{10... | collective-permute-start | bytes 98312 | tf_op jit(solution)/shard_map/ppermute | solution.py:210
  16.1 1.5 %collective-permute-start.6 = (f32[8,1024]{1,0:T(8,128)S(1)}, f32[8,1024]{1,0:T(8,128)S(1)}, u32[]{:S(2)}, u32[]{:S(2)}) collective-permute-start(f32[8,1024]{1,0:T(8,128)S(1)} %theirs.1), channel_id=1, source_target_pairs={{0,1},{1,0},{2,3},{3,2},{4,5},{5,4},{6,7},{7,6},{8,9},{9,8},{10,11... | collective-permute-start | bytes 98312 | tf_op jit(solution)/shard_map/ppermute | solution.py:221

commit v5 on v4

--- a/solution.py
+++ b/solution.py
@@ -10,7 +10,6 @@
 HITS = 2
 VMEM = pl.BlockSpec(memory_space=pltpu.VMEM)
 HBM = pl.BlockSpec(memory_space=pltpu.HBM)
-CHUNKS = 2
 
 
 def call(kernel, name, out_shape, in_specs, scratch=(), flops=0, moved=0):
@@ -112,12 +111,15 @@
         held_ref[core] = tile
 
 
-def merge_kernel(facts_ref, held_ref, got_ref, both_ref, mine_ref):
-    my_core = lax.axis_index("dev") % 2
+def merge_kernel(facts_ref, held_ref, got_ref, both_ref, mine_ref, theirs_ref):
+    my_dev = lax.axis_index("dev")
+    my_core = my_dev % 2
     for core in range(2):
-        here = facts_ref[core : core + 1, 0:1] % 2 == my_core
+        slot = facts_ref[core : core + 1, 0:1]
+        here = (slot % 2 == my_core) == (slot // 2 == my_dev // 2)
         both_ref[core] = jnp.where(here, held_ref[core], got_ref[core])
     mine_ref[...] = both_ref[my_core]
+    theirs_ref[...] = both_ref[1 - my_core]
 
 
 def theirs_kernel(after_ref, both_ref, theirs_ref):
@@ -163,10 +165,18 @@
 
     own = amps[0, 0]
     others = [
-        lax.ppermute(own, "dev", [(i, i ^ k) for i in range(devs)]) for k in range(2, devs, 2)
-    ]
-    half = jax.ShapeDtypeStruct((width, width // 2), jnp.bfloat16)
-    landing = [pltpu.VMEM((width // 2, width), jnp.float32), pltpu.SemaphoreType.DMA((CHUNKS,))]
+        lax.ppermute(own, "dev", [(i, i ^ k) for i in range(devs)]) for k in range(3, devs, 2)
+    ]
+    chunk = width // 4
+
+    def part(chunks):
+        return jax.ShapeDtypeStruct((width, chunks * chunk), jnp.bfloat16), [
+            pltpu.VMEM((chunks * chunk, width), jnp.float32),
+            pltpu.SemaphoreType.DMA((chunks,)),
+        ]
+
+    early, early_landing = part(1)
+    late, late_landing = part(3)
     facts, denom, own, high_a, low_a = call(
         stage_kernel,
         "stage",
@@ -174,8 +184,8 @@
             jax.ShapeDtypeStruct((HITS + nodes, LANES), jnp.int32),
             jax.ShapeDtypeStruct((nodes, groups, LANES), jnp.float32),
             tile,
-            half,
-            half,
+            early,
+            early,
         ),
         [pl.BlockSpec(memory_space=pltpu.SMEM)] + [HBM] * 5,
         [
@@ -183,7 +193,7 @@
             pltpu.VMEM(task_rows.shape, jnp.int32),
             pltpu.VMEM(virt_energy.shape, jnp.float32),
             pltpu.SemaphoreType.DMA((4,)),
-            *landing,
+            *early_landing,
         ],
         flops=width * width,
         moved=4 * width * width,
@@ -193,7 +203,7 @@
     swap = [(i, i ^ 1) for i in range(devs)]
     held = call(pick_kernel, "pick", both, [VMEM] * (1 + len(slots)))(facts, *slots)
     got = lax.ppermute(held, "dev", swap)
-    chip_tiles, mine = call(merge_kernel, "merge", (both, tile), [VMEM] * 3)(facts, held, got)
+    chip_tiles, mine, theirs = call(merge_kernel, "merge", (both, tile, tile), [VMEM] * 3)(facts, held, got)
 
     fetched = [
         lax.ppermute(
@@ -207,13 +217,21 @@
         )
         for k in range(1, nodes - 1, 2)
     ]
-    last = lax.ppermute(mine, "node", [(i, i ^ (nodes - 1)) for i in range(nodes)])
+    last = lax.ppermute(
+        theirs,
+        ("node", "dev"),
+        [
+            (n * devs + d, (n ^ (nodes - 1)) * devs + (d ^ 1))
+            for n in range(nodes)
+            for d in range(devs)
+        ],
+    )
     high_b, low_b = call(
         split_kernel,
         "split",
-        (half, half),
+        (late, late),
         [VMEM, HBM],
-        landing,
+        late_landing,
         flops=width * width,
         moved=4 * width * width,
     )(mine, in_hbm(ints[0, 0]))

time: 31.1 us -> 30.2 us (0.971)
  waiting for transfers between devices: 4.08 us -> 3.42 us
    ppermute x1, waiting for transfers between devices: 1.46 us -> 0.17 us  [on_device(): lax.ppermute(theirs, ('node', 'dev'), [(n * devs + d, (n ^ nodes - 1) * d...]
    ppermute x1, starting transfers between devices: 0.07 us -> 0.79 us  [on_device(): lax.ppermute(call(theirs_kernel, 'theirs', tile, [VMEM] * 2)(high_b, tile...]
    ppermute x1, waiting for transfers between devices: 0.01 us -> 0.69 us  [on_device(): lax.ppermute(call(theirs_kernel, 'theirs', tile, [VMEM] * 2)(high_b, tile...]
    ppermute x1, starting transfers between devices: 2.47 us -> 1.87 us  [on_device(): lax.ppermute(theirs, ('node', 'dev'), [(n * devs + d, (n ^ nodes - 1) * d...]
    pallas_call x2, Pallas kernels: 1.98 us -> 2.33 us  [the longest x1 2.27 us: on_device(): call(split_kernel, 'split', (late, late), [VMEM, HBM], late_landing, flop...]
    pallas_call x1, Pallas kernels: 2.03 us -> 1.68 us  [on_device(): call(stage_kernel, 'stage', (jax.ShapeDtypeStruct((HITS + nodes, LANES),...]
  transfers between devices with their start and end apart: 7 -> 7, of which waited for: 4 -> 5; matrix products, arithmetic and copies ran while one was open for 0% -> 0% of each run, Pallas kernels for 13% -> 13%
where the time goes in v5:
time: 30.2 us; the launch traced here: 30 us
  blocking collectives  11.6 us (38%)
  starting transfers between devices  8.66 us (29%)
  Pallas kernels  4.97 us (16%)
  waiting for transfers between devices  3.42 us (11%)
  between operations  0.72 us (2%)
  other arithmetic  0.63 us (2%)
    all_to_all x1, blocking collectives, on_device(): terms = lax.all_to_all(products, ('node', 'dev'), 0, 0, tiled=True)  11.6 us
    ppermute x3, starting transfers between devices, on_device(): lax.ppermute(own, 'dev', [(i, i ^ k) for i in range(devs)])  4.18 us
    pallas_call x1, Pallas kernels, on_device(): call(split_kernel, 'split', (late, late), [VMEM, HBM], late_landing, flop...  2.27 us
    ppermute x1, starting transfers between devices, on_device(): lax.ppermute(theirs, ('node', 'dev'), [(n * devs + d, (n ^ nodes - 1) * d...  1.87 us
    pallas_call x1, Pallas kernels, on_device(): call(stage_kernel, 'stage', (jax.ShapeDtypeStruct((HITS + nodes, LANES),...  1.68 us
    ppermute x1, starting transfers between devices, on_device(): lax.ppermute(chip_tiles, ('node', 'dev'), [(n * devs + d, (n ^ k + d % 2)...  1.64 us
    ppermute x3, waiting for transfers between devices, on_device(): lax.ppermute(own, 'dev', [(i, i ^ k) for i in range(devs)])  1.42 us
    ppermute x1, waiting for transfers between devices, on_device(): got = lax.ppermute(held, 'dev', swap)  1.14 us
  transfers between devices with their start and end apart: 7, of which 5 were waited for; matrix products, arithmetic and copies ran while one was open for 0% of the time, Pallas kernels for 13%

profile of v5, /device:TPU:0, one launch (start us, length us, event | category | flops | bytes accessed | tf_op | source)
XLA Modules:
  0.0 30.0 jit_solution(71872247444993926)
XLA Ops:
  0.0 3.3 %collective-permute-start.2 = (f32[8,1024]{1,0:T(8,128)}, f32[8,1024]{1,0:T(8,128)S(1)}, u32[]{:S(2)}, u32[]{:S(2)}) collective-permute-start(f32[8,1024]{1,0:T(8,128)} %bitcast.8), channel_id=1, source_target_pairs={{0,7},{1,6},{2,5},{3,4},{4,3},{5,2},{6,1},{7,0},{8,15},{9,14},{10,... | collective-permute-start | bytes 98312 | tf_op jit(solution)/shard_map/ppermute | solution.py:168
  3.3 0.8 %collective-permute-start.1 = (f32[8,1024]{1,0:T(8,128)}, f32[8,1024]{1,0:T(8,128)S(1)}, u32[]{:S(2)}, u32[]{:S(2)}) collective-permute-start(f32[8,1024]{1,0:T(8,128)} %bitcast.9), channel_id=1, source_target_pairs={{0,5},{1,4},{2,7},{3,6},{4,1},{5,0},{6,3},{7,2},{8,13},{9,12},{10,... | collective-permute-start | bytes 98312 | tf_op jit(solution)/shard_map/ppermute | solution.py:168
  4.1 0.1 collective-permute-start
  4.8 1.7 %stage.1 = (s32[6,128]{1,0:T(8,128)S(1)}, f32[4,8,128]{2,1,0:T(8,128)S(1)}, f32[8,1024]{1,0:T(8,128)S(1)}, bf16[1024,256]{1,0:T(8,128)(2,1)S(1)}, bf16[1024,256]{1,0:T(8,128)(2,1)S(1)}) custom-call(f32[1,1]{1,0:T(1,128)S(6)} %copy.7.pair_ref, s32[4,8]{1,0:T(4,128)} %tile_hbm.1, s32[4,2,16]{2,1,0:T(2,128)} %bitcast.12, f32[4,1024]{1,0:T(4,128)} %virt_hbm.1, ...), custom_call_target="tpu_custom_call" | custom-call | flops 1048576 | bytes 4194304 | tf_op jit(solution)/shard_map/stage/pallas_call | solution.py:180
  6.5 0.0 collective-permute-done.2.refs_3_
  6.5 0.4 %collective-permute-done.1.refs_2_ = f32[8,1024]{1,0:T(8,128)S(1)} collective-permute-done((f32[8,1024]{1,0:T(8,128)}, f32[8,1024]{1,0:T(8,128)S(1)}, u32[]{:S(2)}, u32[]{:S(2)}) %collective-permute-start.1) | collective-permute-done | bytes 32800 | tf_op jit(solution)/shard_map/ppermute | solution.py:168
  6.9 1.1 %collective-permute-done.refs_1_ = f32[8,1024]{1,0:T(8,128)S(1)} collective-permute-done((f32[8,1024]{1,0:T(8,128)}, f32[8,1024]{1,0:T(8,128)S(1)}, u32[]{:S(2)}, u32[]{:S(2)}) %collective-permute-start) | collective-permute-done | bytes 32800 | tf_op jit(solution)/shard_map/ppermute | solution.py:168
  8.0 0.1 pick.1.held_ref
  8.0 0.2 collective-permute-start.3
  8.2 1.1 %collective-permute-done.3.got_ref = f32[2,8,1024]{2,1,0:T(8,128)S(1)} collective-permute-done((f32[2,8,1024]{2,1,0:T(8,128)S(1)}, f32[2,8,1024]{2,1,0:T(8,128)S(1)}, u32[]{:S(2)}, u32[]{:S(2)}) %collective-permute-start.3) | collective-permute-done | bytes 65568 | tf_op jit(solution)/shard_map/ppermute | solution.py:205
  9.3 0.1 merge.1
  9.4 1.6 %collective-permute-start.5 = (f32[2,8,1024]{2,1,0:T(8,128)S(1)}, f32[2,8,1024]{2,1,0:T(8,128)S(1)}, u32[]{:S(2)}, u32[]{:S(2)}) collective-permute-start(f32[2,8,1024]{2,1,0:T(8,128)S(1)} %get-tuple-element.23), channel_id=1, source_target_pairs={{0,8},{1,17},{2,10},{3,19},{4,12},{5,21},{6,14},{7,23},{8,0},{9,25... | collective-permute-start | bytes 196616 | tf_op jit(solution)/shard_map/ppermute | solution.py:209
  11.0 1.9 %collective-permute-start.4 = (f32[8,1024]{1,0:T(8,128)S(1)}, f32[8,1024]{1,0:T(8,128)S(1)}, u32[]{:S(2)}, u32[]{:S(2)}) collective-permute-start(f32[8,1024]{1,0:T(8,128)S(1)} %get-tuple-element.22), channel_id=1, source_target_pairs={{0,25},{1,24},{2,27},{3,26},{4,29},{5,28},{6,31},{7,30},{8,17},{9,... | collective-permute-start | bytes 98312 | tf_op jit(solution)/shard_map/ppermute | solution.py:220
  12.9 2.3 %split.1 = (bf16[1024,768]{1,0:T(8,128)(2,1)S(1)}, bf16[1024,768]{1,0:T(8,128)(2,1)S(1)}) custom-call(f32[8,1024]{1,0:T(8,128)S(1)} %get-tuple-element.19.after_ref.mine_ref, f32[1024,1024]{1,0:T(8,128)} %bitcast.7), custom_call_target="tpu_custom_call" | custom-call | flops 1048576 | bytes 4194304 | tf_op jit(solution)/shard_map/split/pallas_call | solution.py:229
  15.2 0.0 collective-permute-done.5.both_ref.refs_0_
  15.2 0.8 %collective-permute-start.6 = (f32[8,1024]{1,0:T(8,128)S(1)}, f32[8,1024]{1,0:T(8,128)S(1)}, u32[]{:S(2)}, u32[]{:S(2)}) collective-permute-start(f32[8,1024]{1,0:T(8,128)S(1)} %theirs.1), channel_id=1, source_target_pairs={{0,1},{1,0},{2,3},{3,2},{4,5},{5,4},{6,7},{7,6},{8,9},{9,8},{10,11... | collective-permute-start | bytes 98312 | tf_op jit(solution)/shard_map/ppermute | solution.py:239
  16.0 0.2 collective-permute-done.4.last_ref
  16.2 0.7 %collective-permute-done.6.refs_1_ = f32[8,1024]{1,0:T(8,128)S(1)} collective-permute-done((f32[8,1024]{1,0:T(8,128)S(1)}, f32[8,1024]{1,0:T(8,128)S(1)}, u32[]{:S(2)}, u32[]{:S(2)}) %collective-permute-start.6) | collective-permute-done | bytes 32800 | tf_op jit(solution)/shard_map/ppermute | solution.py:239
  16.9 0.9 %product.1 = f32[32,8,128]{2,1,0:T(8,128)S(1)} custom-call(s32[6,128]{1,0:T(8,128)S(1)} %get-tuple-element.15.facts_ref, bf16[1024,256]{1,0:T(8,128)(2,1)S(1)} %get-tuple-element.16.high_a_ref, bf16[1024,256]{1,0:T(8,128)(2,1)S(1)} %get-tuple-element.17.low_a_ref, bf16[1024,768]{1,0:T(8,128)(2,1)S(1)} %get-tuple-element.20.after_ref.high_b_ref, ...), custom_call_target="tpu_custom_call" | custom-call | flops 201326592 | bytes 4194304 | tf_op jit(solution)/shard_map/product/pallas_call | solution.py:242
  17.8 11.6 %all_to_all.5 = f32[32,8,128]{2,1,0:T(8,128)S(1)} all-to-all(f32[32,8,128]{2,1,0:T(8,128)S(1)} %product.1), channel_id=1, replica_groups=mesh['node'=4,'dev'=8] {'node','dev'}, dimensions={0} | all-to-all | bytes 262144 | tf_op jit(solution)/shard_map/all_to_all | solution.py:252
  29.4 0.6 %div.3 = f32[4,8,128]{2,1,0:T(8,128)} divide(f32[4,8,128]{2,1,0:T(8,128)S(1)} %bitcast_reduce_fusion, f32[4,8,128]{2,1,0:T(8,128)S(1)} %get-tuple-element.24) | non-fusion elementwise | flops 4096 | bytes 49152 | tf_op jit(solution)/shard_map/div | solution.py:254
  (2 shorter events, 0.0 us)
Async XLA Ops:
  0.0 6.5 %collective-permute-start.2 = (f32[8,1024]{1,0:T(8,128)}, f32[8,1024]{1,0:T(8,128)S(1)}, u32[]{:S(2)}, u32[]{:S(2)}) collective-permute-start(f32[8,1024]{1,0:T(8,128)} %bitcast.8), channel_id=1, source_target_pairs={{0,7},{1,6},{2,5},{3,4},{4,3},{5,2},{6,1},{7,0},{8,15},{9,14},{10,... | collective-permute-start | bytes 98312 | tf_op jit(solution)/shard_map/ppermute | solution.py:168
  3.3 3.6 %collective-permute-start.1 = (f32[8,1024]{1,0:T(8,128)}, f32[8,1024]{1,0:T(8,128)S(1)}, u32[]{:S(2)}, u32[]{:S(2)}) collective-permute-start(f32[8,1024]{1,0:T(8,128)} %bitcast.9), channel_id=1, source_target_pairs={{0,5},{1,4},{2,7},{3,6},{4,1},{5,0},{6,3},{7,2},{8,13},{9,12},{10,... | collective-permute-start | bytes 98312 | tf_op jit(solution)/shard_map/ppermute | solution.py:168
  4.1 3.8 %collective-permute-start = (f32[8,1024]{1,0:T(8,128)}, f32[8,1024]{1,0:T(8,128)S(1)}, u32[]{:S(2)}, u32[]{:S(2)}) collective-permute-start(f32[8,1024]{1,0:T(8,128)} %bitcast.10), channel_id=1, source_target_pairs={{0,3},{1,2},{2,1},{3,0},{4,7},{5,6},{6,5},{7,4},{8,11},{9,10},{10,... | collective-permute-start | bytes 98312 | tf_op jit(solution)/shard_map/ppermute | solution.py:168
  8.0 1.3 %collective-permute-start.3 = (f32[2,8,1024]{2,1,0:T(8,128)S(1)}, f32[2,8,1024]{2,1,0:T(8,128)S(1)}, u32[]{:S(2)}, u32[]{:S(2)}) collective-permute-start(f32[2,8,1024]{2,1,0:T(8,128)S(1)} %pick.1.held_ref), channel_id=1, source_target_pairs={{0,1},{1,0},{2,3},{3,2},{4,5},{5,4},{6,7},{7,6},{8,9},{9,8},{10,11... | collective-permute-start | bytes 196616 | tf_op jit(solution)/shard_map/ppermute | solution.py:205
  9.4 5.8 %collective-permute-start.5 = (f32[2,8,1024]{2,1,0:T(8,128)S(1)}, f32[2,8,1024]{2,1,0:T(8,128)S(1)}, u32[]{:S(2)}, u32[]{:S(2)}) collective-permute-start(f32[2,8,1024]{2,1,0:T(8,128)S(1)} %get-tuple-element.23), channel_id=1, source_target_pairs={{0,8},{1,17},{2,10},{3,19},{4,12},{5,21},{6,14},{7,23},{8,0},{9,25... | collective-permute-start | bytes 196616 | tf_op jit(solution)/shard_map/ppermute | solution.py:209
  11.0 5.1 %collective-permute-start.4 = (f32[8,1024]{1,0:T(8,128)S(1)}, f32[8,1024]{1,0:T(8,128)S(1)}, u32[]{:S(2)}, u32[]{:S(2)}) collective-permute-start(f32[8,1024]{1,0:T(8,128)S(1)} %get-tuple-element.22), channel_id=1, source_target_pairs={{0,25},{1,24},{2,27},{3,26},{4,29},{5,28},{6,31},{7,30},{8,17},{9,... | collective-permute-start | bytes 98312 | tf_op jit(solution)/shard_map/ppermute | solution.py:220
  15.2 1.6 %collective-permute-start.6 = (f32[8,1024]{1,0:T(8,128)S(1)}, f32[8,1024]{1,0:T(8,128)S(1)}, u32[]{:S(2)}, u32[]{:S(2)}) collective-permute-start(f32[8,1024]{1,0:T(8,128)S(1)} %theirs.1), channel_id=1, source_target_pairs={{0,1},{1,0},{2,3},{3,2},{4,5},{5,4},{6,7},{7,6},{8,9},{9,8},{10,11... | collective-permute-start | bytes 98312 | tf_op jit(solution)/shard_map/ppermute | solution.py:239

commit v6 on v5

--- a/solution.py
+++ b/solution.py
@@ -1,3 +1,6 @@
+import functools
+import math
+
 import jax
 import jax.numpy as jnp
 from jax import lax
@@ -10,6 +13,11 @@
 HITS = 2
 VMEM = pl.BlockSpec(memory_space=pltpu.VMEM)
 HBM = pl.BlockSpec(memory_space=pltpu.HBM)
+
+
+def exchange_order(total):
+    step = total - 5 if math.gcd(5, total) == 1 else 1
+    return [(j * step) % total for j in range(total)]
 
 
 def call(kernel, name, out_shape, in_specs, scratch=(), flops=0, moved=0):
@@ -151,9 +159,19 @@
         both = jnp.dot(amp_both, high_ref[...], preferred_element_type=jnp.float32)
         rest = jnp.dot(amp_high, low_ref[...], preferred_element_type=jnp.float32)
         result = both[:total] + (both[total:] + rest)
-        for j in range(high_ref.shape[1] // LANES):
-            out_ref[:, first + j, :] = result[:, j * LANES : (j + 1) * LANES]
+        for position, row in enumerate(exchange_order(total)):
+            for j in range(high_ref.shape[1] // LANES):
+                out_ref[position, first + j, :] = result[row, j * LANES : (j + 1) * LANES]
         first += high_ref.shape[1] // LANES
+
+
+def resid_kernel(devs, terms_ref, denom_ref, resid_ref):
+    sums = [None] * resid_ref.shape[0]
+    for position, device in enumerate(exchange_order(terms_ref.shape[0])):
+        node, term = device // devs, terms_ref[position]
+        sums[node] = term if sums[node] is None else sums[node] + term
+    for node, total in enumerate(sums):
+        resid_ref[node] = total / denom_ref[node]
 
 
 def on_device(amps, amp_tile, ints, tasks, pair_energy, virt_energy):
@@ -249,9 +267,21 @@
         moved=4 * width * width,
     )(facts, high_a, low_a, high_b, low_b, mine, last, *fetched, *handed)
 
-    terms = lax.all_to_all(products, ("node", "dev"), 0, 0, tiled=True)
-    ladder = jnp.sum(terms.reshape(nodes, devs, groups, LANES), axis=1)
-    return (ladder / denom).reshape(1, 1, nodes * width)
+    terms = lax.all_to_all(
+        products,
+        ("node", "dev"),
+        0,
+        0,
+        tiled=True,
+        axis_index_groups=[exchange_order(nodes * devs)],
+    )
+    resid = call(
+        functools.partial(resid_kernel, devs),
+        "resid",
+        jax.ShapeDtypeStruct((nodes, groups, LANES), jnp.float32),
+        [VMEM] * 2,
+    )(terms, denom)
+    return resid.reshape(1, 1, nodes * width)
 
 
 def solution(mesh):

time: 30.2 us -> 29.5 us (0.977)
  blocking collectives: 11.6 us -> 10.9 us
  other arithmetic: 0.63 us -> 0 us
  Pallas kernels: 4.97 us -> 5.58 us
    all_to_all x1, blocking collectives: 11.6 us -> 10.9 us  [on_device(): lax.all_to_all(products, ('node', 'dev'), 0, 0, tiled=True, axis_index_gr...]
    pallas_call x0 -> x1, Pallas kernels: none -> 0.62 us  [on_device(): call(functools.partial(resid_kernel, devs), 'resid', jax.ShapeDtypeStruct...]
    div x1 -> x0, other arithmetic: 0.62 us -> none  [on_device(): return (ladder / denom).reshape(1, 1, nodes * width)]
  transfers between devices with their start and end apart: 7 -> 7, of which waited for: 5 -> 5; matrix products, arithmetic and copies ran while one was open for 0% -> 0% of each run, Pallas kernels for 13% -> 14%
where the time goes in v6:
time: 29.5 us; the launch traced here: 29.3 us
  blocking collectives  10.9 us (37%)
  starting transfers between devices  8.66 us (29%)
  Pallas kernels  5.58 us (19%)
  waiting for transfers between devices  3.42 us (12%)
  between operations  0.72 us (2%)
    all_to_all x1, blocking collectives, on_device(): lax.all_to_all(products, ('node', 'dev'), 0, 0, tiled=True, axis_index_gr...  10.9 us
    ppermute x3, starting transfers between devices, on_device(): lax.ppermute(own, 'dev', [(i, i ^ k) for i in range(devs)])  4.18 us
    pallas_call x1, Pallas kernels, on_device(): call(split_kernel, 'split', (late, late), [VMEM, HBM], late_landing, flop...  2.27 us
    ppermute x1, starting transfers between devices, on_device(): lax.ppermute(theirs, ('node', 'dev'), [(n * devs + d, (n ^ nodes - 1) * d...  1.87 us
    pallas_call x1, Pallas kernels, on_device(): call(stage_kernel, 'stage', (jax.ShapeDtypeStruct((HITS + nodes, LANES),...  1.68 us
    ppermute x1, starting transfers between devices, on_device(): lax.ppermute(chip_tiles, ('node', 'dev'), [(n * devs + d, (n ^ k + d % 2)...  1.64 us
    ppermute x3, waiting for transfers between devices, on_device(): lax.ppermute(own, 'dev', [(i, i ^ k) for i in range(devs)])  1.42 us
    ppermute x1, waiting for transfers between devices, on_device(): got = lax.ppermute(held, 'dev', swap)  1.14 us
  transfers between devices with their start and end apart: 7, of which 5 were waited for; matrix products, arithmetic and copies ran while one was open for 0% of the time, Pallas kernels for 14%

profile of v6, /device:TPU:0, one launch (start us, length us, event | category | flops | bytes accessed | tf_op | source)
XLA Modules:
  0.0 29.3 jit_solution(15617267440473313562)
XLA Ops:
  0.0 3.3 %collective-permute-start.2 = (f32[8,1024]{1,0:T(8,128)}, f32[8,1024]{1,0:T(8,128)S(1)}, u32[]{:S(2)}, u32[]{:S(2)}) collective-permute-start(f32[8,1024]{1,0:T(8,128)} %bitcast.6), channel_id=1, source_target_pairs={{0,7},{1,6},{2,5},{3,4},{4,3},{5,2},{6,1},{7,0},{8,15},{9,14},{10,... | collective-permute-start | bytes 98312 | tf_op jit(solution)/shard_map/ppermute | solution.py:186
  3.3 0.8 %collective-permute-start.1 = (f32[8,1024]{1,0:T(8,128)}, f32[8,1024]{1,0:T(8,128)S(1)}, u32[]{:S(2)}, u32[]{:S(2)}) collective-permute-start(f32[8,1024]{1,0:T(8,128)} %bitcast.7), channel_id=1, source_target_pairs={{0,5},{1,4},{2,7},{3,6},{4,1},{5,0},{6,3},{7,2},{8,13},{9,12},{10,... | collective-permute-start | bytes 98312 | tf_op jit(solution)/shard_map/ppermute | solution.py:186
  4.1 0.1 collective-permute-start
  4.8 1.7 %stage.1 = (s32[6,128]{1,0:T(8,128)S(1)}, f32[4,8,128]{2,1,0:T(8,128)S(1)}, f32[8,1024]{1,0:T(8,128)S(1)}, bf16[1024,256]{1,0:T(8,128)(2,1)S(1)}, bf16[1024,256]{1,0:T(8,128)(2,1)S(1)}) custom-call(f32[1,1]{1,0:T(1,128)S(6)} %copy.7.pair_ref, s32[4,8]{1,0:T(4,128)} %tile_hbm.1, s32[4,2,16]{2,1,0:T(2,128)} %bitcast.10, f32[4,1024]{1,0:T(4,128)} %virt_hbm.1, ...), custom_call_target="tpu_custom_call" | custom-call | flops 1048576 | bytes 4194304 | tf_op jit(solution)/shard_map/stage/pallas_call | solution.py:198
  6.5 0.0 collective-permute-done.2.refs_3_
  6.5 0.4 %collective-permute-done.1.refs_2_ = f32[8,1024]{1,0:T(8,128)S(1)} collective-permute-done((f32[8,1024]{1,0:T(8,128)}, f32[8,1024]{1,0:T(8,128)S(1)}, u32[]{:S(2)}, u32[]{:S(2)}) %collective-permute-start.1) | collective-permute-done | bytes 32800 | tf_op jit(solution)/shard_map/ppermute | solution.py:186
  6.9 1.1 %collective-permute-done.refs_1_ = f32[8,1024]{1,0:T(8,128)S(1)} collective-permute-done((f32[8,1024]{1,0:T(8,128)}, f32[8,1024]{1,0:T(8,128)S(1)}, u32[]{:S(2)}, u32[]{:S(2)}) %collective-permute-start) | collective-permute-done | bytes 32800 | tf_op jit(solution)/shard_map/ppermute | solution.py:186
  8.0 0.1 pick.1.held_ref
  8.0 0.2 collective-permute-start.3
  8.2 1.1 %collective-permute-done.3.got_ref = f32[2,8,1024]{2,1,0:T(8,128)S(1)} collective-permute-done((f32[2,8,1024]{2,1,0:T(8,128)S(1)}, f32[2,8,1024]{2,1,0:T(8,128)S(1)}, u32[]{:S(2)}, u32[]{:S(2)}) %collective-permute-start.3) | collective-permute-done | bytes 65568 | tf_op jit(solution)/shard_map/ppermute | solution.py:223
  9.3 0.1 merge.1
  9.4 1.6 %collective-permute-start.5 = (f32[2,8,1024]{2,1,0:T(8,128)S(1)}, f32[2,8,1024]{2,1,0:T(8,128)S(1)}, u32[]{:S(2)}, u32[]{:S(2)}) collective-permute-start(f32[2,8,1024]{2,1,0:T(8,128)S(1)} %get-tuple-element.23), channel_id=1, source_target_pairs={{0,8},{1,17},{2,10},{3,19},{4,12},{5,21},{6,14},{7,23},{8,0},{9,25... | collective-permute-start | bytes 196616 | tf_op jit(solution)/shard_map/ppermute | solution.py:227
  11.0 1.9 %collective-permute-start.4 = (f32[8,1024]{1,0:T(8,128)S(1)}, f32[8,1024]{1,0:T(8,128)S(1)}, u32[]{:S(2)}, u32[]{:S(2)}) collective-permute-start(f32[8,1024]{1,0:T(8,128)S(1)} %get-tuple-element.22), channel_id=1, source_target_pairs={{0,25},{1,24},{2,27},{3,26},{4,29},{5,28},{6,31},{7,30},{8,17},{9,... | collective-permute-start | bytes 98312 | tf_op jit(solution)/shard_map/ppermute | solution.py:238
  12.9 2.3 %split.1 = (bf16[1024,768]{1,0:T(8,128)(2,1)S(1)}, bf16[1024,768]{1,0:T(8,128)(2,1)S(1)}) custom-call(f32[8,1024]{1,0:T(8,128)S(1)} %get-tuple-element.19.after_ref.mine_ref, f32[1024,1024]{1,0:T(8,128)} %bitcast.5), custom_call_target="tpu_custom_call" | custom-call | flops 1048576 | bytes 4194304 | tf_op jit(solution)/shard_map/split/pallas_call | solution.py:247
  15.2 0.0 collective-permute-done.5.both_ref.refs_0_
  15.2 0.8 %collective-permute-start.6 = (f32[8,1024]{1,0:T(8,128)S(1)}, f32[8,1024]{1,0:T(8,128)S(1)}, u32[]{:S(2)}, u32[]{:S(2)}) collective-permute-start(f32[8,1024]{1,0:T(8,128)S(1)} %theirs.1), channel_id=1, source_target_pairs={{0,1},{1,0},{2,3},{3,2},{4,5},{5,4},{6,7},{7,6},{8,9},{9,8},{10,11... | collective-permute-start | bytes 98312 | tf_op jit(solution)/shard_map/ppermute | solution.py:257
  16.0 0.2 collective-permute-done.4.last_ref
  16.2 0.7 %collective-permute-done.6.refs_1_ = f32[8,1024]{1,0:T(8,128)S(1)} collective-permute-done((f32[8,1024]{1,0:T(8,128)S(1)}, f32[8,1024]{1,0:T(8,128)S(1)}, u32[]{:S(2)}, u32[]{:S(2)}) %collective-permute-start.6) | collective-permute-done | bytes 32800 | tf_op jit(solution)/shard_map/ppermute | solution.py:257
  16.9 0.9 %product.1 = f32[32,8,128]{2,1,0:T(8,128)S(1)} custom-call(s32[6,128]{1,0:T(8,128)S(1)} %get-tuple-element.15.facts_ref, bf16[1024,256]{1,0:T(8,128)(2,1)S(1)} %get-tuple-element.16.high_a_ref, bf16[1024,256]{1,0:T(8,128)(2,1)S(1)} %get-tuple-element.17.low_a_ref, bf16[1024,768]{1,0:T(8,128)(2,1)S(1)} %get-tuple-element.20.after_ref.high_b_ref, ...), custom_call_target="tpu_custom_call" | custom-call | flops 201326592 | bytes 4194304 | tf_op jit(solution)/shard_map/product/pallas_call | solution.py:260
  17.8 10.9 %all_to_all.5.terms_ref = f32[32,8,128]{2,1,0:T(8,128)S(1)} all-to-all(f32[32,8,128]{2,1,0:T(8,128)S(1)} %product.1), channel_id=1, replica_groups={{0,27,22,17,12,7,2,29,24,19,14,9,4,31,26,21,16,11,6,1,28,23,18,13,8,3,3..., dimensions={0} | all-to-all | bytes 262144 | tf_op jit(solution)/shard_map/all_to_all | solution.py:270
  28.7 0.6 %resid.1 = f32[4,8,128]{2,1,0:T(8,128)} custom-call(f32[32,8,128]{2,1,0:T(8,128)S(1)} %all_to_all.5.terms_ref, f32[4,8,128]{2,1,0:T(8,128)S(1)} %get-tuple-element.24.denom_ref), custom_call_target="tpu_custom_call" | custom-call | tf_op jit(solution)/shard_map/resid/pallas_call | solution.py:278
  (1 shorter events, 0.0 us)
Async XLA Ops:
  0.0 6.5 %collective-permute-start.2 = (f32[8,1024]{1,0:T(8,128)}, f32[8,1024]{1,0:T(8,128)S(1)}, u32[]{:S(2)}, u32[]{:S(2)}) collective-permute-start(f32[8,1024]{1,0:T(8,128)} %bitcast.6), channel_id=1, source_target_pairs={{0,7},{1,6},{2,5},{3,4},{4,3},{5,2},{6,1},{7,0},{8,15},{9,14},{10,... | collective-permute-start | bytes 98312 | tf_op jit(solution)/shard_map/ppermute | solution.py:186
  3.3 3.6 %collective-permute-start.1 = (f32[8,1024]{1,0:T(8,128)}, f32[8,1024]{1,0:T(8,128)S(1)}, u32[]{:S(2)}, u32[]{:S(2)}) collective-permute-start(f32[8,1024]{1,0:T(8,128)} %bitcast.7), channel_id=1, source_target_pairs={{0,5},{1,4},{2,7},{3,6},{4,1},{5,0},{6,3},{7,2},{8,13},{9,12},{10,... | collective-permute-start | bytes 98312 | tf_op jit(solution)/shard_map/ppermute | solution.py:186
  4.1 3.8 %collective-permute-start = (f32[8,1024]{1,0:T(8,128)}, f32[8,1024]{1,0:T(8,128)S(1)}, u32[]{:S(2)}, u32[]{:S(2)}) collective-permute-start(f32[8,1024]{1,0:T(8,128)} %bitcast.8), channel_id=1, source_target_pairs={{0,3},{1,2},{2,1},{3,0},{4,7},{5,6},{6,5},{7,4},{8,11},{9,10},{10,... | collective-permute-start | bytes 98312 | tf_op jit(solution)/shard_map/ppermute | solution.py:186
  8.0 1.3 %collective-permute-start.3 = (f32[2,8,1024]{2,1,0:T(8,128)S(1)}, f32[2,8,1024]{2,1,0:T(8,128)S(1)}, u32[]{:S(2)}, u32[]{:S(2)}) collective-permute-start(f32[2,8,1024]{2,1,0:T(8,128)S(1)} %pick.1.held_ref), channel_id=1, source_target_pairs={{0,1},{1,0},{2,3},{3,2},{4,5},{5,4},{6,7},{7,6},{8,9},{9,8},{10,11... | collective-permute-start | bytes 196616 | tf_op jit(solution)/shard_map/ppermute | solution.py:223
  9.4 5.8 %collective-permute-start.5 = (f32[2,8,1024]{2,1,0:T(8,128)S(1)}, f32[2,8,1024]{2,1,0:T(8,128)S(1)}, u32[]{:S(2)}, u32[]{:S(2)}) collective-permute-start(f32[2,8,1024]{2,1,0:T(8,128)S(1)} %get-tuple-element.23), channel_id=1, source_target_pairs={{0,8},{1,17},{2,10},{3,19},{4,12},{5,21},{6,14},{7,23},{8,0},{9,25... | collective-permute-start | bytes 196616 | tf_op jit(solution)/shard_map/ppermute | solution.py:227
  11.0 5.1 %collective-permute-start.4 = (f32[8,1024]{1,0:T(8,128)S(1)}, f32[8,1024]{1,0:T(8,128)S(1)}, u32[]{:S(2)}, u32[]{:S(2)}) collective-permute-start(f32[8,1024]{1,0:T(8,128)S(1)} %get-tuple-element.22), channel_id=1, source_target_pairs={{0,25},{1,24},{2,27},{3,26},{4,29},{5,28},{6,31},{7,30},{8,17},{9,... | collective-permute-start | bytes 98312 | tf_op jit(solution)/shard_map/ppermute | solution.py:238
  15.2 1.6 %collective-permute-start.6 = (f32[8,1024]{1,0:T(8,128)S(1)}, f32[8,1024]{1,0:T(8,128)S(1)}, u32[]{:S(2)}, u32[]{:S(2)}) collective-permute-start(f32[8,1024]{1,0:T(8,128)S(1)} %theirs.1), channel_id=1, source_target_pairs={{0,1},{1,0},{2,3},{3,2},{4,5},{5,4},{6,7},{7,6},{8,9},{9,8},{10,11... | collective-permute-start | bytes 98312 | tf_op jit(solution)/shard_map/ppermute | solution.py:257

commit v7 on v6

--- a/solution.py
+++ b/solution.py
@@ -18,6 +18,12 @@
 def exchange_order(total):
     step = total - 5 if math.gcd(5, total) == 1 else 1
     return [(j * step) % total for j in range(total)]
+
+
+def gather_steps(devs):
+    odd = list(range(1, devs // 2))
+    even = odd[1::-1] + odd[2:]
+    return list(zip(even, odd))
 
 
 def call(kernel, name, out_shape, in_specs, scratch=(), flops=0, moved=0):
@@ -108,14 +114,17 @@
     split_rows(ints_hbm, ints_hbm.shape[0] - high_ref.shape[1], land_ref, sems, high_ref, low_ref)()
 
 
-def pick_kernel(facts_ref, *refs):
+def pick_kernel(facts_ref, own_ref, *refs):
     pieces, held_ref = refs[:-1], refs[-1]
-    chip = lax.axis_index("dev") // 2
+    my_dev = lax.axis_index("dev")
+    steps = [
+        jnp.where(my_dev % 2 == 0, odd, even) for even, odd in gather_steps(2 * len(pieces) + 2)
+    ]
     for core in range(2):
-        step = (facts_ref[core : core + 1, 0:1] // 2) ^ chip
-        tile = pieces[0][...]
-        for j, piece in enumerate(pieces[1:], 1):
-            tile = jnp.where(step == j, piece[...], tile)
+        wanted = (facts_ref[core : core + 1, 0:1] // 2) ^ (my_dev // 2)
+        tile = own_ref[...]
+        for step, piece in zip(steps, pieces):
+            tile = jnp.where(wanted == step, piece[...], tile)
         held_ref[core] = tile
 
 
@@ -183,7 +192,8 @@
 
     own = amps[0, 0]
     others = [
-        lax.ppermute(own, "dev", [(i, i ^ k) for i in range(devs)]) for k in range(3, devs, 2)
+        lax.ppermute(own, "dev", [(i, i ^ (2 * steps[i % 2] + 1)) for i in range(devs)])
+        for steps in gather_steps(devs)
     ]
     chunk = width // 4
 
@@ -216,10 +226,9 @@
         flops=width * width,
         moved=4 * width * width,
     )(pair_energy, *map(in_hbm, (amp_tile, task_rows, virt_energy, own, ints[0, 0])))
-    slots = [own, *others]
     both = jax.ShapeDtypeStruct((2, pairs, width), jnp.float32)
     swap = [(i, i ^ 1) for i in range(devs)]
-    held = call(pick_kernel, "pick", both, [VMEM] * (1 + len(slots)))(facts, *slots)
+    held = call(pick_kernel, "pick", both, [VMEM] * (2 + len(others)))(facts, own, *others)
     got = lax.ppermute(held, "dev", swap)
     chip_tiles, mine, theirs = call(merge_kernel, "merge", (both, tile, tile), [VMEM] * 3)(facts, held, got)
 

time: 29.5 us -> 29.1 us (0.986)
  starting transfers between devices: 8.66 us -> 9.57 us
  waiting for transfers between devices: 3.42 us -> 2.56 us
  blocking collectives: 10.9 us -> 10.5 us
    ppermute x3, starting transfers between devices: 4.18 us -> 5.08 us  [on_device(): lax.ppermute(own, 'dev', [(i, i ^ 2 * steps[i % 2] + 1) for i in range(de...]
    ppermute x3, waiting for transfers between devices: 1.42 us -> 0.57 us  [on_device(): lax.ppermute(own, 'dev', [(i, i ^ 2 * steps[i % 2] + 1) for i in range(de...]
    all_to_all x1, blocking collectives: 10.9 us -> 10.5 us  [on_device(): lax.all_to_all(products, ('node', 'dev'), 0, 0, tiled=True, axis_index_gr...]
  transfers between devices with their start and end apart: 7 -> 7, of which waited for: 5 -> 4; matrix products, arithmetic and copies ran while one was open for 0% -> 0% of each run, Pallas kernels for 14% -> 14%
where the time goes in v7:
time: 29.1 us; the launch traced here: 29 us
  blocking collectives  10.5 us (36%)
  starting transfers between devices  9.57 us (33%)
  Pallas kernels  5.58 us (19%)
  waiting for transfers between devices  2.56 us (9%)
  between operations  0.73 us (3%)
    all_to_all x1, blocking collectives, on_device(): lax.all_to_all(products, ('node', 'dev'), 0, 0, tiled=True, axis_index_gr...  10.5 us
    ppermute x3, starting transfers between devices, on_device(): lax.ppermute(own, 'dev', [(i, i ^ 2 * steps[i % 2] + 1) for i in range(de...  5.08 us
    pallas_call x1, Pallas kernels, on_device(): call(split_kernel, 'split', (late, late), [VMEM, HBM], late_landing, flop...  2.27 us
    ppermute x1, starting transfers between devices, on_device(): lax.ppermute(theirs, ('node', 'dev'), [(n * devs + d, (n ^ nodes - 1) * d...  1.87 us
    pallas_call x1, Pallas kernels, on_device(): call(stage_kernel, 'stage', (jax.ShapeDtypeStruct((HITS + nodes, LANES),...  1.68 us
    ppermute x1, starting transfers between devices, on_device(): lax.ppermute(chip_tiles, ('node', 'dev'), [(n * devs + d, (n ^ k + d % 2)...  1.64 us
    ppermute x1, waiting for transfers between devices, on_device(): got = lax.ppermute(held, 'dev', swap)  1.13 us
    pallas_call x1, Pallas kernels, on_device(): call(product_kernel, 'product', jax.ShapeDtypeStruct((nodes * pairs, grou...  0.88 us
  transfers between devices with their start and end apart: 7, of which 4 were waited for; matrix products, arithmetic and copies ran while one was open for 0% of the time, Pallas kernels for 14%

profile of v7, /device:TPU:0, one launch (start us, length us, event | category | flops | bytes accessed | tf_op | source)
XLA Modules:
  0.0 29.0 jit_solution(4664466577314601382)
XLA Ops:
  0.0 3.3 %collective-permute-start.2 = (f32[8,1024]{1,0:T(8,128)}, f32[8,1024]{1,0:T(8,128)S(1)}, u32[]{:S(2)}, u32[]{:S(2)}) collective-permute-start(f32[8,1024]{1,0:T(8,128)} %bitcast.6), channel_id=1, source_target_pairs={{0,7},{1,6},{2,5},{3,4},{4,3},{5,2},{6,1},{7,0},{8,15},{9,14},{10,... | collective-permute-start | bytes 98312 | tf_op jit(solution)/shard_map/ppermute | solution.py:195
  3.3 0.8 %collective-permute-start.1 = (f32[8,1024]{1,0:T(8,128)}, f32[8,1024]{1,0:T(8,128)S(1)}, u32[]{:S(2)}, u32[]{:S(2)}) collective-permute-start(f32[8,1024]{1,0:T(8,128)} %bitcast.7), channel_id=1, source_target_pairs={{0,3},{1,4},{2,1},{3,6},{4,7},{5,0},{6,5},{7,2},{8,11},{9,12},{10,... | collective-permute-start | bytes 98312 | tf_op jit(solution)/shard_map/ppermute | solution.py:195
  4.2 0.9 %collective-permute-start = (f32[8,1024]{1,0:T(8,128)}, f32[8,1024]{1,0:T(8,128)S(1)}, u32[]{:S(2)}, u32[]{:S(2)}) collective-permute-start(f32[8,1024]{1,0:T(8,128)} %bitcast.8), channel_id=1, source_target_pairs={{0,5},{1,2},{2,7},{3,0},{4,1},{5,6},{6,3},{7,4},{8,13},{9,10},{10,... | collective-permute-start | bytes 98312 | tf_op jit(solution)/shard_map/ppermute | solution.py:195
  5.7 1.7 %stage.1 = (s32[6,128]{1,0:T(8,128)S(1)}, f32[4,8,128]{2,1,0:T(8,128)S(1)}, f32[8,1024]{1,0:T(8,128)S(1)}, bf16[1024,256]{1,0:T(8,128)(2,1)S(1)}, bf16[1024,256]{1,0:T(8,128)(2,1)S(1)}) custom-call(f32[1,1]{1,0:T(1,128)S(6)} %copy.7.pair_ref, s32[4,8]{1,0:T(4,128)} %tile_hbm.1, s32[4,2,16]{2,1,0:T(2,128)} %bitcast.10, f32[4,1024]{1,0:T(4,128)} %virt_hbm.1, ...), custom_call_target="tpu_custom_call" | custom-call | flops 1048576 | bytes 4194304 | tf_op jit(solution)/shard_map/stage/pallas_call | solution.py:208
  7.4 0.0 collective-permute-done.2.refs_2_
  7.4 0.0 collective-permute-done.1.refs_1_
  7.4 0.6 %collective-permute-done.refs_0_ = f32[8,1024]{1,0:T(8,128)S(1)} collective-permute-done((f32[8,1024]{1,0:T(8,128)}, f32[8,1024]{1,0:T(8,128)S(1)}, u32[]{:S(2)}, u32[]{:S(2)}) %collective-permute-start) | collective-permute-done | bytes 32800 | tf_op jit(solution)/shard_map/ppermute | solution.py:195
  8.0 0.1 pick.1.held_ref
  8.1 0.2 collective-permute-start.3
  8.3 1.1 %collective-permute-done.3.got_ref = f32[2,8,1024]{2,1,0:T(8,128)S(1)} collective-permute-done((f32[2,8,1024]{2,1,0:T(8,128)S(1)}, f32[2,8,1024]{2,1,0:T(8,128)S(1)}, u32[]{:S(2)}, u32[]{:S(2)}) %collective-permute-start.3) | collective-permute-done | bytes 65568 | tf_op jit(solution)/shard_map/ppermute | solution.py:232
  9.4 0.1 merge.1
  9.5 1.6 %collective-permute-start.5 = (f32[2,8,1024]{2,1,0:T(8,128)S(1)}, f32[2,8,1024]{2,1,0:T(8,128)S(1)}, u32[]{:S(2)}, u32[]{:S(2)}) collective-permute-start(f32[2,8,1024]{2,1,0:T(8,128)S(1)} %get-tuple-element.23), channel_id=1, source_target_pairs={{0,8},{1,17},{2,10},{3,19},{4,12},{5,21},{6,14},{7,23},{8,0},{9,25... | collective-permute-start | bytes 196616 | tf_op jit(solution)/shard_map/ppermute | solution.py:236
  11.1 1.9 %collective-permute-start.4 = (f32[8,1024]{1,0:T(8,128)S(1)}, f32[8,1024]{1,0:T(8,128)S(1)}, u32[]{:S(2)}, u32[]{:S(2)}) collective-permute-start(f32[8,1024]{1,0:T(8,128)S(1)} %get-tuple-element.22), channel_id=1, source_target_pairs={{0,25},{1,24},{2,27},{3,26},{4,29},{5,28},{6,31},{7,30},{8,17},{9,... | collective-permute-start | bytes 98312 | tf_op jit(solution)/shard_map/ppermute | solution.py:247
  13.0 2.3 %split.1 = (bf16[1024,768]{1,0:T(8,128)(2,1)S(1)}, bf16[1024,768]{1,0:T(8,128)(2,1)S(1)}) custom-call(f32[8,1024]{1,0:T(8,128)S(1)} %get-tuple-element.19.after_ref.mine_ref, f32[1024,1024]{1,0:T(8,128)} %bitcast.5), custom_call_target="tpu_custom_call" | custom-call | flops 1048576 | bytes 4194304 | tf_op jit(solution)/shard_map/split/pallas_call | solution.py:256
  15.2 0.0 collective-permute-done.5.both_ref.refs_0_
  15.3 0.8 %collective-permute-start.6 = (f32[8,1024]{1,0:T(8,128)S(1)}, f32[8,1024]{1,0:T(8,128)S(1)}, u32[]{:S(2)}, u32[]{:S(2)}) collective-permute-start(f32[8,1024]{1,0:T(8,128)S(1)} %theirs.1), channel_id=1, source_target_pairs={{0,1},{1,0},{2,3},{3,2},{4,5},{5,4},{6,7},{7,6},{8,9},{9,8},{10,11... | collective-permute-start | bytes 98312 | tf_op jit(solution)/shard_map/ppermute | solution.py:266
  16.1 0.2 collective-permute-done.4.last_ref
  16.2 0.7 %collective-permute-done.6.refs_1_ = f32[8,1024]{1,0:T(8,128)S(1)} collective-permute-done((f32[8,1024]{1,0:T(8,128)S(1)}, f32[8,1024]{1,0:T(8,128)S(1)}, u32[]{:S(2)}, u32[]{:S(2)}) %collective-permute-start.6) | collective-permute-done | bytes 32800 | tf_op jit(solution)/shard_map/ppermute | solution.py:266
  16.9 0.9 %product.1 = f32[32,8,128]{2,1,0:T(8,128)S(1)} custom-call(s32[6,128]{1,0:T(8,128)S(1)} %get-tuple-element.15.facts_ref, bf16[1024,256]{1,0:T(8,128)(2,1)S(1)} %get-tuple-element.16.high_a_ref, bf16[1024,256]{1,0:T(8,128)(2,1)S(1)} %get-tuple-element.17.low_a_ref, bf16[1024,768]{1,0:T(8,128)(2,1)S(1)} %get-tuple-element.20.after_ref.high_b_ref, ...), custom_call_target="tpu_custom_call" | custom-call | flops 201326592 | bytes 4194304 | tf_op jit(solution)/shard_map/product/pallas_call | solution.py:269
  17.8 10.5 %all_to_all.5.terms_ref = f32[32,8,128]{2,1,0:T(8,128)S(1)} all-to-all(f32[32,8,128]{2,1,0:T(8,128)S(1)} %product.1), channel_id=1, replica_groups={{0,27,22,17,12,7,2,29,24,19,14,9,4,31,26,21,16,11,6,1,28,23,18,13,8,3,3..., dimensions={0} | all-to-all | bytes 262144 | tf_op jit(solution)/shard_map/all_to_all | solution.py:279
  28.3 0.6 %resid.1 = f32[4,8,128]{2,1,0:T(8,128)} custom-call(f32[32,8,128]{2,1,0:T(8,128)S(1)} %all_to_all.5.terms_ref, f32[4,8,128]{2,1,0:T(8,128)S(1)} %get-tuple-element.24.denom_ref), custom_call_target="tpu_custom_call" | custom-call | tf_op jit(solution)/shard_map/resid/pallas_call | solution.py:287
  (1 shorter events, 0.0 us)
Async XLA Ops:
  0.0 7.4 %collective-permute-start.2 = (f32[8,1024]{1,0:T(8,128)}, f32[8,1024]{1,0:T(8,128)S(1)}, u32[]{:S(2)}, u32[]{:S(2)}) collective-permute-start(f32[8,1024]{1,0:T(8,128)} %bitcast.6), channel_id=1, source_target_pairs={{0,7},{1,6},{2,5},{3,4},{4,3},{5,2},{6,1},{7,0},{8,15},{9,14},{10,... | collective-permute-start | bytes 98312 | tf_op jit(solution)/shard_map/ppermute | solution.py:195
  3.3 4.1 %collective-permute-start.1 = (f32[8,1024]{1,0:T(8,128)}, f32[8,1024]{1,0:T(8,128)S(1)}, u32[]{:S(2)}, u32[]{:S(2)}) collective-permute-start(f32[8,1024]{1,0:T(8,128)} %bitcast.7), channel_id=1, source_target_pairs={{0,3},{1,4},{2,1},{3,6},{4,7},{5,0},{6,5},{7,2},{8,11},{9,12},{10,... | collective-permute-start | bytes 98312 | tf_op jit(solution)/shard_map/ppermute | solution.py:195
  4.2 3.9 %collective-permute-start = (f32[8,1024]{1,0:T(8,128)}, f32[8,1024]{1,0:T(8,128)S(1)}, u32[]{:S(2)}, u32[]{:S(2)}) collective-permute-start(f32[8,1024]{1,0:T(8,128)} %bitcast.8), channel_id=1, source_target_pairs={{0,5},{1,2},{2,7},{3,0},{4,1},{5,6},{6,3},{7,4},{8,13},{9,10},{10,... | collective-permute-start | bytes 98312 | tf_op jit(solution)/shard_map/ppermute | solution.py:195
  8.1 1.3 %collective-permute-start.3 = (f32[2,8,1024]{2,1,0:T(8,128)S(1)}, f32[2,8,1024]{2,1,0:T(8,128)S(1)}, u32[]{:S(2)}, u32[]{:S(2)}) collective-permute-start(f32[2,8,1024]{2,1,0:T(8,128)S(1)} %pick.1.held_ref), channel_id=1, source_target_pairs={{0,1},{1,0},{2,3},{3,2},{4,5},{5,4},{6,7},{7,6},{8,9},{9,8},{10,11... | collective-permute-start | bytes 196616 | tf_op jit(solution)/shard_map/ppermute | solution.py:232
  9.5 5.8 %collective-permute-start.5 = (f32[2,8,1024]{2,1,0:T(8,128)S(1)}, f32[2,8,1024]{2,1,0:T(8,128)S(1)}, u32[]{:S(2)}, u32[]{:S(2)}) collective-permute-start(f32[2,8,1024]{2,1,0:T(8,128)S(1)} %get-tuple-element.23), channel_id=1, source_target_pairs={{0,8},{1,17},{2,10},{3,19},{4,12},{5,21},{6,14},{7,23},{8,0},{9,25... | collective-permute-start | bytes 196616 | tf_op jit(solution)/shard_map/ppermute | solution.py:236
  11.1 5.1 %collective-permute-start.4 = (f32[8,1024]{1,0:T(8,128)S(1)}, f32[8,1024]{1,0:T(8,128)S(1)}, u32[]{:S(2)}, u32[]{:S(2)}) collective-permute-start(f32[8,1024]{1,0:T(8,128)S(1)} %get-tuple-element.22), channel_id=1, source_target_pairs={{0,25},{1,24},{2,27},{3,26},{4,29},{5,28},{6,31},{7,30},{8,17},{9,... | collective-permute-start | bytes 98312 | tf_op jit(solution)/shard_map/ppermute | solution.py:247
  15.3 1.6 %collective-permute-start.6 = (f32[8,1024]{1,0:T(8,128)S(1)}, f32[8,1024]{1,0:T(8,128)S(1)}, u32[]{:S(2)}, u32[]{:S(2)}) collective-permute-start(f32[8,1024]{1,0:T(8,128)S(1)} %theirs.1), channel_id=1, source_target_pairs={{0,1},{1,0},{2,3},{3,2},{4,5},{5,4},{6,7},{7,6},{8,9},{9,8},{10,11... | collective-permute-start | bytes 98312 | tf_op jit(solution)/shard_map/ppermute | solution.py:266

commit v8 on v7

--- a/solution.py
+++ b/solution.py
@@ -103,7 +103,7 @@
         hit = jnp.where((task[0:1] == my_node) & (task[1:2] == my_dev), 1, 0)
         hit = jnp.max(hit, axis=1, keepdims=True)
         facts_ref[HITS + k : HITS + k + 1, :] = jnp.broadcast_to(hit, (1, LANES))
-    denom = pair_ref[0, 0] - virt_ref[...]
+    denom = pair_ref[...] - virt_ref[...]
     for j in range(denom_ref.shape[1]):
         denom_ref[:, j, :] = denom[:, j * LANES : (j + 1) * LANES]
     finish()
@@ -215,7 +215,7 @@
             early,
             early,
         ),
-        [pl.BlockSpec(memory_space=pltpu.SMEM)] + [HBM] * 5,
+        [VMEM] + [HBM] * 5,
         [
             pltpu.VMEM(amp_tile.shape, jnp.int32),
             pltpu.VMEM(task_rows.shape, jnp.int32),

time: 29.1 us -> 29.1 us (level)
  no operation moved by 1% of the time
where the time goes in v8:
time: 29.1 us; the launch traced here: 29 us
  blocking collectives  10.5 us (36%)
  starting transfers between devices  9.57 us (33%)
  Pallas kernels  5.58 us (19%)
  waiting for transfers between devices  2.56 us (9%)
  between operations  0.73 us (3%)
    all_to_all x1, blocking collectives, on_device(): lax.all_to_all(products, ('node', 'dev'), 0, 0, tiled=True, axis_index_gr...  10.5 us
    ppermute x3, starting transfers between devices, on_device(): lax.ppermute(own, 'dev', [(i, i ^ 2 * steps[i % 2] + 1) for i in range(de...  5.08 us
    pallas_call x1, Pallas kernels, on_device(): call(split_kernel, 'split', (late, late), [VMEM, HBM], late_landing, flop...  2.27 us
    ppermute x1, starting transfers between devices, on_device(): lax.ppermute(theirs, ('node', 'dev'), [(n * devs + d, (n ^ nodes - 1) * d...  1.87 us
    pallas_call x1, Pallas kernels, on_device(): call(stage_kernel, 'stage', (jax.ShapeDtypeStruct((HITS + nodes, LANES),...  1.68 us
    ppermute x1, starting transfers between devices, on_device(): lax.ppermute(chip_tiles, ('node', 'dev'), [(n * devs + d, (n ^ k + d % 2)...  1.64 us
    ppermute x1, waiting for transfers between devices, on_device(): got = lax.ppermute(held, 'dev', swap)  1.13 us
    pallas_call x1, Pallas kernels, on_device(): call(product_kernel, 'product', jax.ShapeDtypeStruct((nodes * pairs, grou...  0.88 us
  transfers between devices with their start and end apart: 7, of which 4 were waited for; matrix products, arithmetic and copies ran while one was open for 0% of the time, Pallas kernels for 14%

profile of v8, /device:TPU:0, one launch (start us, length us, event | category | flops | bytes accessed | tf_op | source)
XLA Modules:
  0.0 29.0 jit_solution(8382084639718748325)
XLA Ops:
  0.0 3.3 %collective-permute-start.2 = (f32[8,1024]{1,0:T(8,128)}, f32[8,1024]{1,0:T(8,128)S(1)}, u32[]{:S(2)}, u32[]{:S(2)}) collective-permute-start(f32[8,1024]{1,0:T(8,128)} %bitcast.6), channel_id=1, source_target_pairs={{0,7},{1,6},{2,5},{3,4},{4,3},{5,2},{6,1},{7,0},{8,15},{9,14},{10,... | collective-permute-start | bytes 98312 | tf_op jit(solution)/shard_map/ppermute | solution.py:195
  3.3 0.8 %collective-permute-start.1 = (f32[8,1024]{1,0:T(8,128)}, f32[8,1024]{1,0:T(8,128)S(1)}, u32[]{:S(2)}, u32[]{:S(2)}) collective-permute-start(f32[8,1024]{1,0:T(8,128)} %bitcast.7), channel_id=1, source_target_pairs={{0,3},{1,4},{2,1},{3,6},{4,7},{5,0},{6,5},{7,2},{8,11},{9,12},{10,... | collective-permute-start | bytes 98312 | tf_op jit(solution)/shard_map/ppermute | solution.py:195
  4.2 0.9 %collective-permute-start = (f32[8,1024]{1,0:T(8,128)}, f32[8,1024]{1,0:T(8,128)S(1)}, u32[]{:S(2)}, u32[]{:S(2)}) collective-permute-start(f32[8,1024]{1,0:T(8,128)} %bitcast.8), channel_id=1, source_target_pairs={{0,5},{1,2},{2,7},{3,0},{4,1},{5,6},{6,3},{7,4},{8,13},{9,10},{10,... | collective-permute-start | bytes 98312 | tf_op jit(solution)/shard_map/ppermute | solution.py:195
  5.7 1.7 %stage.1 = (s32[6,128]{1,0:T(8,128)S(1)}, f32[4,8,128]{2,1,0:T(8,128)S(1)}, f32[8,1024]{1,0:T(8,128)S(1)}, bf16[1024,256]{1,0:T(8,128)(2,1)S(1)}, bf16[1024,256]{1,0:T(8,128)(2,1)S(1)}) custom-call(f32[1,1]{1,0:T(1,128)S(6)} %copy.7.pair_ref, s32[4,8]{1,0:T(4,128)} %tile_hbm.1, s32[4,2,16]{2,1,0:T(2,128)} %bitcast.10, f32[4,1024]{1,0:T(4,128)} %virt_hbm.1, ...), custom_call_target="tpu_custom_call" | custom-call | flops 1048576 | bytes 4194304 | tf_op jit(solution)/shard_map/stage/pallas_call | solution.py:208
  7.4 0.0 collective-permute-done.2.refs_2_
  7.4 0.0 collective-permute-done.1.refs_1_
  7.4 0.6 %collective-permute-done.refs_0_ = f32[8,1024]{1,0:T(8,128)S(1)} collective-permute-done((f32[8,1024]{1,0:T(8,128)}, f32[8,1024]{1,0:T(8,128)S(1)}, u32[]{:S(2)}, u32[]{:S(2)}) %collective-permute-start) | collective-permute-done | bytes 32800 | tf_op jit(solution)/shard_map/ppermute | solution.py:195
  8.0 0.1 pick.1.held_ref
  8.1 0.2 collective-permute-start.3
  8.3 1.1 %collective-permute-done.3.got_ref = f32[2,8,1024]{2,1,0:T(8,128)S(1)} collective-permute-done((f32[2,8,1024]{2,1,0:T(8,128)S(1)}, f32[2,8,1024]{2,1,0:T(8,128)S(1)}, u32[]{:S(2)}, u32[]{:S(2)}) %collective-permute-start.3) | collective-permute-done | bytes 65568 | tf_op jit(solution)/shard_map/ppermute | solution.py:232
  9.4 0.1 merge.1
  9.5 1.6 %collective-permute-start.5 = (f32[2,8,1024]{2,1,0:T(8,128)S(1)}, f32[2,8,1024]{2,1,0:T(8,128)S(1)}, u32[]{:S(2)}, u32[]{:S(2)}) collective-permute-start(f32[2,8,1024]{2,1,0:T(8,128)S(1)} %get-tuple-element.23), channel_id=1, source_target_pairs={{0,8},{1,17},{2,10},{3,19},{4,12},{5,21},{6,14},{7,23},{8,0},{9,25... | collective-permute-start | bytes 196616 | tf_op jit(solution)/shard_map/ppermute | solution.py:236
  11.1 1.9 %collective-permute-start.4 = (f32[8,1024]{1,0:T(8,128)S(1)}, f32[8,1024]{1,0:T(8,128)S(1)}, u32[]{:S(2)}, u32[]{:S(2)}) collective-permute-start(f32[8,1024]{1,0:T(8,128)S(1)} %get-tuple-element.22), channel_id=1, source_target_pairs={{0,25},{1,24},{2,27},{3,26},{4,29},{5,28},{6,31},{7,30},{8,17},{9,... | collective-permute-start | bytes 98312 | tf_op jit(solution)/shard_map/ppermute | solution.py:247
  13.0 2.3 %split.1 = (bf16[1024,768]{1,0:T(8,128)(2,1)S(1)}, bf16[1024,768]{1,0:T(8,128)(2,1)S(1)}) custom-call(f32[8,1024]{1,0:T(8,128)S(1)} %get-tuple-element.19.after_ref.mine_ref, f32[1024,1024]{1,0:T(8,128)} %bitcast.5), custom_call_target="tpu_custom_call" | custom-call | flops 1048576 | bytes 4194304 | tf_op jit(solution)/shard_map/split/pallas_call | solution.py:256
  15.2 0.0 collective-permute-done.5.both_ref.refs_0_
  15.3 0.8 %collective-permute-start.6 = (f32[8,1024]{1,0:T(8,128)S(1)}, f32[8,1024]{1,0:T(8,128)S(1)}, u32[]{:S(2)}, u32[]{:S(2)}) collective-permute-start(f32[8,1024]{1,0:T(8,128)S(1)} %theirs.1), channel_id=1, source_target_pairs={{0,1},{1,0},{2,3},{3,2},{4,5},{5,4},{6,7},{7,6},{8,9},{9,8},{10,11... | collective-permute-start | bytes 98312 | tf_op jit(solution)/shard_map/ppermute | solution.py:266
  16.1 0.2 collective-permute-done.4.last_ref
  16.2 0.7 %collective-permute-done.6.refs_1_ = f32[8,1024]{1,0:T(8,128)S(1)} collective-permute-done((f32[8,1024]{1,0:T(8,128)S(1)}, f32[8,1024]{1,0:T(8,128)S(1)}, u32[]{:S(2)}, u32[]{:S(2)}) %collective-permute-start.6) | collective-permute-done | bytes 32800 | tf_op jit(solution)/shard_map/ppermute | solution.py:266
  16.9 0.9 %product.1 = f32[32,8,128]{2,1,0:T(8,128)S(1)} custom-call(s32[6,128]{1,0:T(8,128)S(1)} %get-tuple-element.15.facts_ref, bf16[1024,256]{1,0:T(8,128)(2,1)S(1)} %get-tuple-element.16.high_a_ref, bf16[1024,256]{1,0:T(8,128)(2,1)S(1)} %get-tuple-element.17.low_a_ref, bf16[1024,768]{1,0:T(8,128)(2,1)S(1)} %get-tuple-element.20.after_ref.high_b_ref, ...), custom_call_target="tpu_custom_call" | custom-call | flops 201326592 | bytes 4194304 | tf_op jit(solution)/shard_map/product/pallas_call | solution.py:269
  17.8 10.5 %all_to_all.5.terms_ref = f32[32,8,128]{2,1,0:T(8,128)S(1)} all-to-all(f32[32,8,128]{2,1,0:T(8,128)S(1)} %product.1), channel_id=1, replica_groups={{0,27,22,17,12,7,2,29,24,19,14,9,4,31,26,21,16,11,6,1,28,23,18,13,8,3,3..., dimensions={0} | all-to-all | bytes 262144 | tf_op jit(solution)/shard_map/all_to_all | solution.py:279
  28.3 0.6 %resid.1 = f32[4,8,128]{2,1,0:T(8,128)} custom-call(f32[32,8,128]{2,1,0:T(8,128)S(1)} %all_to_all.5.terms_ref, f32[4,8,128]{2,1,0:T(8,128)S(1)} %get-tuple-element.24.denom_ref), custom_call_target="tpu_custom_call" | custom-call | tf_op jit(solution)/shard_map/resid/pallas_call | solution.py:287
  (1 shorter events, 0.0 us)
Async XLA Ops:
  0.0 7.4 %collective-permute-start.2 = (f32[8,1024]{1,0:T(8,128)}, f32[8,1024]{1,0:T(8,128)S(1)}, u32[]{:S(2)}, u32[]{:S(2)}) collective-permute-start(f32[8,1024]{1,0:T(8,128)} %bitcast.6), channel_id=1, source_target_pairs={{0,7},{1,6},{2,5},{3,4},{4,3},{5,2},{6,1},{7,0},{8,15},{9,14},{10,... | collective-permute-start | bytes 98312 | tf_op jit(solution)/shard_map/ppermute | solution.py:195
  3.3 4.1 %collective-permute-start.1 = (f32[8,1024]{1,0:T(8,128)}, f32[8,1024]{1,0:T(8,128)S(1)}, u32[]{:S(2)}, u32[]{:S(2)}) collective-permute-start(f32[8,1024]{1,0:T(8,128)} %bitcast.7), channel_id=1, source_target_pairs={{0,3},{1,4},{2,1},{3,6},{4,7},{5,0},{6,5},{7,2},{8,11},{9,12},{10,... | collective-permute-start | bytes 98312 | tf_op jit(solution)/shard_map/ppermute | solution.py:195
  4.2 3.9 %collective-permute-start = (f32[8,1024]{1,0:T(8,128)}, f32[8,1024]{1,0:T(8,128)S(1)}, u32[]{:S(2)}, u32[]{:S(2)}) collective-permute-start(f32[8,1024]{1,0:T(8,128)} %bitcast.8), channel_id=1, source_target_pairs={{0,5},{1,2},{2,7},{3,0},{4,1},{5,6},{6,3},{7,4},{8,13},{9,10},{10,... | collective-permute-start | bytes 98312 | tf_op jit(solution)/shard_map/ppermute | solution.py:195
  8.1 1.3 %collective-permute-start.3 = (f32[2,8,1024]{2,1,0:T(8,128)S(1)}, f32[2,8,1024]{2,1,0:T(8,128)S(1)}, u32[]{:S(2)}, u32[]{:S(2)}) collective-permute-start(f32[2,8,1024]{2,1,0:T(8,128)S(1)} %pick.1.held_ref), channel_id=1, source_target_pairs={{0,1},{1,0},{2,3},{3,2},{4,5},{5,4},{6,7},{7,6},{8,9},{9,8},{10,11... | collective-permute-start | bytes 196616 | tf_op jit(solution)/shard_map/ppermute | solution.py:232
  9.5 5.8 %collective-permute-start.5 = (f32[2,8,1024]{2,1,0:T(8,128)S(1)}, f32[2,8,1024]{2,1,0:T(8,128)S(1)}, u32[]{:S(2)}, u32[]{:S(2)}) collective-permute-start(f32[2,8,1024]{2,1,0:T(8,128)S(1)} %get-tuple-element.23), channel_id=1, source_target_pairs={{0,8},{1,17},{2,10},{3,19},{4,12},{5,21},{6,14},{7,23},{8,0},{9,25... | collective-permute-start | bytes 196616 | tf_op jit(solution)/shard_map/ppermute | solution.py:236
  11.1 5.1 %collective-permute-start.4 = (f32[8,1024]{1,0:T(8,128)S(1)}, f32[8,1024]{1,0:T(8,128)S(1)}, u32[]{:S(2)}, u32[]{:S(2)}) collective-permute-start(f32[8,1024]{1,0:T(8,128)S(1)} %get-tuple-element.22), channel_id=1, source_target_pairs={{0,25},{1,24},{2,27},{3,26},{4,29},{5,28},{6,31},{7,30},{8,17},{9,... | collective-permute-start | bytes 98312 | tf_op jit(solution)/shard_map/ppermute | solution.py:247
  15.3 1.6 %collective-permute-start.6 = (f32[8,1024]{1,0:T(8,128)S(1)}, f32[8,1024]{1,0:T(8,128)S(1)}, u32[]{:S(2)}, u32[]{:S(2)}) collective-permute-start(f32[8,1024]{1,0:T(8,128)S(1)} %theirs.1), channel_id=1, source_target_pairs={{0,1},{1,0},{2,3},{3,2},{4,5},{5,4},{6,7},{7,6},{8,9},{9,8},{10,11... | collective-permute-start | bytes 98312 | tf_op jit(solution)/shard_map/ppermute | solution.py:266

commit v9 on v7

--- a/solution.py
+++ b/solution.py
@@ -54,7 +54,7 @@
         for i in range(chunks)
     ]
     for copy in copies:
-        copy.start()
+        copy.start(priority=1)
 
     def finish():
         for i, copy in enumerate(copies):

time: 29.1 us -> 29.1 us (level)
  no operation moved by 1% of the time
where the time goes in v9:
time: 29.1 us; the launch traced here: 29 us
  blocking collectives  10.5 us (36%)
  starting transfers between devices  9.56 us (33%)
  Pallas kernels  5.57 us (19%)
  waiting for transfers between devices  2.57 us (9%)
  between operations  0.73 us (3%)
    all_to_all x1, blocking collectives, on_device(): lax.all_to_all(products, ('node', 'dev'), 0, 0, tiled=True, axis_index_gr...  10.5 us
    ppermute x3, starting transfers between devices, on_device(): lax.ppermute(own, 'dev', [(i, i ^ 2 * steps[i % 2] + 1) for i in range(de...  5.08 us
    pallas_call x1, Pallas kernels, on_device(): call(split_kernel, 'split', (late, late), [VMEM, HBM], late_landing, flop...  2.27 us
    ppermute x1, starting transfers between devices, on_device(): lax.ppermute(theirs, ('node', 'dev'), [(n * devs + d, (n ^ nodes - 1) * d...  1.87 us
    pallas_call x1, Pallas kernels, on_device(): call(stage_kernel, 'stage', (jax.ShapeDtypeStruct((HITS + nodes, LANES),...  1.67 us
    ppermute x1, starting transfers between devices, on_device(): lax.ppermute(chip_tiles, ('node', 'dev'), [(n * devs + d, (n ^ k + d % 2)...  1.64 us
    ppermute x1, waiting for transfers between devices, on_device(): got = lax.ppermute(held, 'dev', swap)  1.13 us
    pallas_call x1, Pallas kernels, on_device(): call(product_kernel, 'product', jax.ShapeDtypeStruct((nodes * pairs, grou...  0.87 us
  transfers between devices with their start and end apart: 7, of which 4 were waited for; matrix products, arithmetic and copies ran while one was open for 0% of the time, Pallas kernels for 14%

profile of v9, /device:TPU:0, one launch (start us, length us, event | category | flops | bytes accessed | tf_op | source)
XLA Modules:
  0.0 29.0 jit_solution(7792160087467652747)
XLA Ops:
  0.0 3.3 %collective-permute-start.2 = (f32[8,1024]{1,0:T(8,128)}, f32[8,1024]{1,0:T(8,128)S(1)}, u32[]{:S(2)}, u32[]{:S(2)}) collective-permute-start(f32[8,1024]{1,0:T(8,128)} %bitcast.6), channel_id=1, source_target_pairs={{0,7},{1,6},{2,5},{3,4},{4,3},{5,2},{6,1},{7,0},{8,15},{9,14},{10,... | collective-permute-start | bytes 98312 | tf_op jit(solution)/shard_map/ppermute | solution.py:195
  3.3 0.8 %collective-permute-start.1 = (f32[8,1024]{1,0:T(8,128)}, f32[8,1024]{1,0:T(8,128)S(1)}, u32[]{:S(2)}, u32[]{:S(2)}) collective-permute-start(f32[8,1024]{1,0:T(8,128)} %bitcast.7), channel_id=1, source_target_pairs={{0,3},{1,4},{2,1},{3,6},{4,7},{5,0},{6,5},{7,2},{8,11},{9,12},{10,... | collective-permute-start | bytes 98312 | tf_op jit(solution)/shard_map/ppermute | solution.py:195
  4.2 0.9 %collective-permute-start = (f32[8,1024]{1,0:T(8,128)}, f32[8,1024]{1,0:T(8,128)S(1)}, u32[]{:S(2)}, u32[]{:S(2)}) collective-permute-start(f32[8,1024]{1,0:T(8,128)} %bitcast.8), channel_id=1, source_target_pairs={{0,5},{1,2},{2,7},{3,0},{4,1},{5,6},{6,3},{7,4},{8,13},{9,10},{10,... | collective-permute-start | bytes 98312 | tf_op jit(solution)/shard_map/ppermute | solution.py:195
  5.7 1.7 %stage.1 = (s32[6,128]{1,0:T(8,128)S(1)}, f32[4,8,128]{2,1,0:T(8,128)S(1)}, f32[8,1024]{1,0:T(8,128)S(1)}, bf16[1024,256]{1,0:T(8,128)(2,1)S(1)}, bf16[1024,256]{1,0:T(8,128)(2,1)S(1)}) custom-call(f32[1,1]{1,0:T(1,128)S(6)} %copy.7.pair_ref, s32[4,8]{1,0:T(4,128)} %tile_hbm.1, s32[4,2,16]{2,1,0:T(2,128)} %bitcast.10, f32[4,1024]{1,0:T(4,128)} %virt_hbm.1, ...), custom_call_target="tpu_custom_call" | custom-call | flops 1048576 | bytes 4194304 | tf_op jit(solution)/shard_map/stage/pallas_call | solution.py:208
  7.4 0.0 collective-permute-done.2.refs_2_
  7.4 0.0 collective-permute-done.1.refs_1_
  7.4 0.6 %collective-permute-done.refs_0_ = f32[8,1024]{1,0:T(8,128)S(1)} collective-permute-done((f32[8,1024]{1,0:T(8,128)}, f32[8,1024]{1,0:T(8,128)S(1)}, u32[]{:S(2)}, u32[]{:S(2)}) %collective-permute-start) | collective-permute-done | bytes 32800 | tf_op jit(solution)/shard_map/ppermute | solution.py:195
  8.0 0.1 pick.1.held_ref
  8.1 0.2 collective-permute-start.3
  8.3 1.1 %collective-permute-done.3.got_ref = f32[2,8,1024]{2,1,0:T(8,128)S(1)} collective-permute-done((f32[2,8,1024]{2,1,0:T(8,128)S(1)}, f32[2,8,1024]{2,1,0:T(8,128)S(1)}, u32[]{:S(2)}, u32[]{:S(2)}) %collective-permute-start.3) | collective-permute-done | bytes 65568 | tf_op jit(solution)/shard_map/ppermute | solution.py:232
  9.4 0.1 merge.1
  9.5 1.6 %collective-permute-start.5 = (f32[2,8,1024]{2,1,0:T(8,128)S(1)}, f32[2,8,1024]{2,1,0:T(8,128)S(1)}, u32[]{:S(2)}, u32[]{:S(2)}) collective-permute-start(f32[2,8,1024]{2,1,0:T(8,128)S(1)} %get-tuple-element.23), channel_id=1, source_target_pairs={{0,8},{1,17},{2,10},{3,19},{4,12},{5,21},{6,14},{7,23},{8,0},{9,25... | collective-permute-start | bytes 196616 | tf_op jit(solution)/shard_map/ppermute | solution.py:236
  11.1 1.9 %collective-permute-start.4 = (f32[8,1024]{1,0:T(8,128)S(1)}, f32[8,1024]{1,0:T(8,128)S(1)}, u32[]{:S(2)}, u32[]{:S(2)}) collective-permute-start(f32[8,1024]{1,0:T(8,128)S(1)} %get-tuple-element.22), channel_id=1, source_target_pairs={{0,25},{1,24},{2,27},{3,26},{4,29},{5,28},{6,31},{7,30},{8,17},{9,... | collective-permute-start | bytes 98312 | tf_op jit(solution)/shard_map/ppermute | solution.py:247
  13.0 2.3 %split.1 = (bf16[1024,768]{1,0:T(8,128)(2,1)S(1)}, bf16[1024,768]{1,0:T(8,128)(2,1)S(1)}) custom-call(f32[8,1024]{1,0:T(8,128)S(1)} %get-tuple-element.19.after_ref.mine_ref, f32[1024,1024]{1,0:T(8,128)} %bitcast.5), custom_call_target="tpu_custom_call" | custom-call | flops 1048576 | bytes 4194304 | tf_op jit(solution)/shard_map/split/pallas_call | solution.py:256
  15.2 0.0 collective-permute-done.5.both_ref.refs_0_
  15.3 0.8 %collective-permute-start.6 = (f32[8,1024]{1,0:T(8,128)S(1)}, f32[8,1024]{1,0:T(8,128)S(1)}, u32[]{:S(2)}, u32[]{:S(2)}) collective-permute-start(f32[8,1024]{1,0:T(8,128)S(1)} %theirs.1), channel_id=1, source_target_pairs={{0,1},{1,0},{2,3},{3,2},{4,5},{5,4},{6,7},{7,6},{8,9},{9,8},{10,11... | collective-permute-start | bytes 98312 | tf_op jit(solution)/shard_map/ppermute | solution.py:266
  16.1 0.2 collective-permute-done.4.last_ref
  16.2 0.7 %collective-permute-done.6.refs_1_ = f32[8,1024]{1,0:T(8,128)S(1)} collective-permute-done((f32[8,1024]{1,0:T(8,128)S(1)}, f32[8,1024]{1,0:T(8,128)S(1)}, u32[]{:S(2)}, u32[]{:S(2)}) %collective-permute-start.6) | collective-permute-done | bytes 32800 | tf_op jit(solution)/shard_map/ppermute | solution.py:266
  16.9 0.9 %product.1 = f32[32,8,128]{2,1,0:T(8,128)S(1)} custom-call(s32[6,128]{1,0:T(8,128)S(1)} %get-tuple-element.15.facts_ref, bf16[1024,256]{1,0:T(8,128)(2,1)S(1)} %get-tuple-element.16.high_a_ref, bf16[1024,256]{1,0:T(8,128)(2,1)S(1)} %get-tuple-element.17.low_a_ref, bf16[1024,768]{1,0:T(8,128)(2,1)S(1)} %get-tuple-element.20.after_ref.high_b_ref, ...), custom_call_target="tpu_custom_call" | custom-call | flops 201326592 | bytes 4194304 | tf_op jit(solution)/shard_map/product/pallas_call | solution.py:269
  17.8 10.5 %all_to_all.5.terms_ref = f32[32,8,128]{2,1,0:T(8,128)S(1)} all-to-all(f32[32,8,128]{2,1,0:T(8,128)S(1)} %product.1), channel_id=1, replica_groups={{0,27,22,17,12,7,2,29,24,19,14,9,4,31,26,21,16,11,6,1,28,23,18,13,8,3,3..., dimensions={0} | all-to-all | bytes 262144 | tf_op jit(solution)/shard_map/all_to_all | solution.py:279
  28.3 0.6 %resid.1 = f32[4,8,128]{2,1,0:T(8,128)} custom-call(f32[32,8,128]{2,1,0:T(8,128)S(1)} %all_to_all.5.terms_ref, f32[4,8,128]{2,1,0:T(8,128)S(1)} %get-tuple-element.24.denom_ref), custom_call_target="tpu_custom_call" | custom-call | tf_op jit(solution)/shard_map/resid/pallas_call | solution.py:287
  (1 shorter events, 0.0 us)
Async XLA Ops:
  0.0 7.4 %collective-permute-start.2 = (f32[8,1024]{1,0:T(8,128)}, f32[8,1024]{1,0:T(8,128)S(1)}, u32[]{:S(2)}, u32[]{:S(2)}) collective-permute-start(f32[8,1024]{1,0:T(8,128)} %bitcast.6), channel_id=1, source_target_pairs={{0,7},{1,6},{2,5},{3,4},{4,3},{5,2},{6,1},{7,0},{8,15},{9,14},{10,... | collective-permute-start | bytes 98312 | tf_op jit(solution)/shard_map/ppermute | solution.py:195
  3.3 4.1 %collective-permute-start.1 = (f32[8,1024]{1,0:T(8,128)}, f32[8,1024]{1,0:T(8,128)S(1)}, u32[]{:S(2)}, u32[]{:S(2)}) collective-permute-start(f32[8,1024]{1,0:T(8,128)} %bitcast.7), channel_id=1, source_target_pairs={{0,3},{1,4},{2,1},{3,6},{4,7},{5,0},{6,5},{7,2},{8,11},{9,12},{10,... | collective-permute-start | bytes 98312 | tf_op jit(solution)/shard_map/ppermute | solution.py:195
  4.2 3.9 %collective-permute-start = (f32[8,1024]{1,0:T(8,128)}, f32[8,1024]{1,0:T(8,128)S(1)}, u32[]{:S(2)}, u32[]{:S(2)}) collective-permute-start(f32[8,1024]{1,0:T(8,128)} %bitcast.8), channel_id=1, source_target_pairs={{0,5},{1,2},{2,7},{3,0},{4,1},{5,6},{6,3},{7,4},{8,13},{9,10},{10,... | collective-permute-start | bytes 98312 | tf_op jit(solution)/shard_map/ppermute | solution.py:195
  8.1 1.3 %collective-permute-start.3 = (f32[2,8,1024]{2,1,0:T(8,128)S(1)}, f32[2,8,1024]{2,1,0:T(8,128)S(1)}, u32[]{:S(2)}, u32[]{:S(2)}) collective-permute-start(f32[2,8,1024]{2,1,0:T(8,128)S(1)} %pick.1.held_ref), channel_id=1, source_target_pairs={{0,1},{1,0},{2,3},{3,2},{4,5},{5,4},{6,7},{7,6},{8,9},{9,8},{10,11... | collective-permute-start | bytes 196616 | tf_op jit(solution)/shard_map/ppermute | solution.py:232
  9.5 5.8 %collective-permute-start.5 = (f32[2,8,1024]{2,1,0:T(8,128)S(1)}, f32[2,8,1024]{2,1,0:T(8,128)S(1)}, u32[]{:S(2)}, u32[]{:S(2)}) collective-permute-start(f32[2,8,1024]{2,1,0:T(8,128)S(1)} %get-tuple-element.23), channel_id=1, source_target_pairs={{0,8},{1,17},{2,10},{3,19},{4,12},{5,21},{6,14},{7,23},{8,0},{9,25... | collective-permute-start | bytes 196616 | tf_op jit(solution)/shard_map/ppermute | solution.py:236
  11.1 5.1 %collective-permute-start.4 = (f32[8,1024]{1,0:T(8,128)S(1)}, f32[8,1024]{1,0:T(8,128)S(1)}, u32[]{:S(2)}, u32[]{:S(2)}) collective-permute-start(f32[8,1024]{1,0:T(8,128)S(1)} %get-tuple-element.22), channel_id=1, source_target_pairs={{0,25},{1,24},{2,27},{3,26},{4,29},{5,28},{6,31},{7,30},{8,17},{9,... | collective-permute-start | bytes 98312 | tf_op jit(solution)/shard_map/ppermute | solution.py:247
  15.3 1.6 %collective-permute-start.6 = (f32[8,1024]{1,0:T(8,128)S(1)}, f32[8,1024]{1,0:T(8,128)S(1)}, u32[]{:S(2)}, u32[]{:S(2)}) collective-permute-start(f32[8,1024]{1,0:T(8,128)S(1)} %theirs.1), channel_id=1, source_target_pairs={{0,1},{1,0},{2,3},{3,2},{4,5},{5,4},{6,7},{7,6},{8,9},{9,8},{10,11... | collective-permute-start | bytes 98312 | tf_op jit(solution)/shard_map/ppermute | solution.py:266

commit v10 on v8

--- a/solution.py
+++ b/solution.py
@@ -54,7 +54,7 @@
         for i in range(chunks)
     ]
     for copy in copies:
-        copy.start()
+        copy.start(priority=1)
 
     def finish():
         for i, copy in enumerate(copies):

time: 29.1 us -> 29.1 us (level)
  no operation moved by 1% of the time
where the time goes in v10:
time: 29.1 us; the launch traced here: 29 us
  blocking collectives  10.5 us (36%)
  starting transfers between devices  9.56 us (33%)
  Pallas kernels  5.58 us (19%)
  waiting for transfers between devices  2.57 us (9%)
  between operations  0.73 us (3%)
    all_to_all x1, blocking collectives, on_device(): lax.all_to_all(products, ('node', 'dev'), 0, 0, tiled=True, axis_index_gr...  10.5 us
    ppermute x3, starting transfers between devices, on_device(): lax.ppermute(own, 'dev', [(i, i ^ 2 * steps[i % 2] + 1) for i in range(de...  5.08 us
    pallas_call x1, Pallas kernels, on_device(): call(split_kernel, 'split', (late, late), [VMEM, HBM], late_landing, flop...  2.27 us
    ppermute x1, starting transfers between devices, on_device(): lax.ppermute(theirs, ('node', 'dev'), [(n * devs + d, (n ^ nodes - 1) * d...  1.87 us
    pallas_call x1, Pallas kernels, on_device(): call(stage_kernel, 'stage', (jax.ShapeDtypeStruct((HITS + nodes, LANES),...  1.67 us
    ppermute x1, starting transfers between devices, on_device(): lax.ppermute(chip_tiles, ('node', 'dev'), [(n * devs + d, (n ^ k + d % 2)...  1.64 us
    ppermute x1, waiting for transfers between devices, on_device(): got = lax.ppermute(held, 'dev', swap)  1.13 us
    pallas_call x1, Pallas kernels, on_device(): call(product_kernel, 'product', jax.ShapeDtypeStruct((nodes * pairs, grou...  0.88 us
  transfers between devices with their start and end apart: 7, of which 4 were waited for; matrix products, arithmetic and copies ran while one was open for 0% of the time, Pallas kernels for 14%

profile of v10, /device:TPU:0, one launch (start us, length us, event | category | flops | bytes accessed | tf_op | source)
XLA Modules:
  0.0 29.0 jit_solution(9999043702012440275)
XLA Ops:
  0.0 3.3 %collective-permute-start.2 = (f32[8,1024]{1,0:T(8,128)}, f32[8,1024]{1,0:T(8,128)S(1)}, u32[]{:S(2)}, u32[]{:S(2)}) collective-permute-start(f32[8,1024]{1,0:T(8,128)} %bitcast.6), channel_id=1, source_target_pairs={{0,7},{1,6},{2,5},{3,4},{4,3},{5,2},{6,1},{7,0},{8,15},{9,14},{10,... | collective-permute-start | bytes 98312 | tf_op jit(solution)/shard_map/ppermute | solution.py:195
  3.3 0.8 %collective-permute-start.1 = (f32[8,1024]{1,0:T(8,128)}, f32[8,1024]{1,0:T(8,128)S(1)}, u32[]{:S(2)}, u32[]{:S(2)}) collective-permute-start(f32[8,1024]{1,0:T(8,128)} %bitcast.7), channel_id=1, source_target_pairs={{0,3},{1,4},{2,1},{3,6},{4,7},{5,0},{6,5},{7,2},{8,11},{9,12},{10,... | collective-permute-start | bytes 98312 | tf_op jit(solution)/shard_map/ppermute | solution.py:195
  4.2 0.9 %collective-permute-start = (f32[8,1024]{1,0:T(8,128)}, f32[8,1024]{1,0:T(8,128)S(1)}, u32[]{:S(2)}, u32[]{:S(2)}) collective-permute-start(f32[8,1024]{1,0:T(8,128)} %bitcast.8), channel_id=1, source_target_pairs={{0,5},{1,2},{2,7},{3,0},{4,1},{5,6},{6,3},{7,4},{8,13},{9,10},{10,... | collective-permute-start | bytes 98312 | tf_op jit(solution)/shard_map/ppermute | solution.py:195
  5.7 1.7 %stage.1 = (s32[6,128]{1,0:T(8,128)S(1)}, f32[4,8,128]{2,1,0:T(8,128)S(1)}, f32[8,1024]{1,0:T(8,128)S(1)}, bf16[1024,256]{1,0:T(8,128)(2,1)S(1)}, bf16[1024,256]{1,0:T(8,128)(2,1)S(1)}) custom-call(f32[1,1]{1,0:T(1,128)S(6)} %copy.7.pair_ref, s32[4,8]{1,0:T(4,128)} %tile_hbm.1, s32[4,2,16]{2,1,0:T(2,128)} %bitcast.10, f32[4,1024]{1,0:T(4,128)} %virt_hbm.1, ...), custom_call_target="tpu_custom_call" | custom-call | flops 1048576 | bytes 4194304 | tf_op jit(solution)/shard_map/stage/pallas_call | solution.py:208
  7.4 0.0 collective-permute-done.2.refs_2_
  7.4 0.0 collective-permute-done.1.refs_1_
  7.4 0.6 %collective-permute-done.refs_0_ = f32[8,1024]{1,0:T(8,128)S(1)} collective-permute-done((f32[8,1024]{1,0:T(8,128)}, f32[8,1024]{1,0:T(8,128)S(1)}, u32[]{:S(2)}, u32[]{:S(2)}) %collective-permute-start) | collective-permute-done | bytes 32800 | tf_op jit(solution)/shard_map/ppermute | solution.py:195
  8.0 0.1 pick.1.held_ref
  8.1 0.2 collective-permute-start.3
  8.3 1.1 %collective-permute-done.3.got_ref = f32[2,8,1024]{2,1,0:T(8,128)S(1)} collective-permute-done((f32[2,8,1024]{2,1,0:T(8,128)S(1)}, f32[2,8,1024]{2,1,0:T(8,128)S(1)}, u32[]{:S(2)}, u32[]{:S(2)}) %collective-permute-start.3) | collective-permute-done | bytes 65568 | tf_op jit(solution)/shard_map/ppermute | solution.py:232
  9.4 0.1 merge.1
  9.5 1.6 %collective-permute-start.5 = (f32[2,8,1024]{2,1,0:T(8,128)S(1)}, f32[2,8,1024]{2,1,0:T(8,128)S(1)}, u32[]{:S(2)}, u32[]{:S(2)}) collective-permute-start(f32[2,8,1024]{2,1,0:T(8,128)S(1)} %get-tuple-element.23), channel_id=1, source_target_pairs={{0,8},{1,17},{2,10},{3,19},{4,12},{5,21},{6,14},{7,23},{8,0},{9,25... | collective-permute-start | bytes 196616 | tf_op jit(solution)/shard_map/ppermute | solution.py:236
  11.1 1.9 %collective-permute-start.4 = (f32[8,1024]{1,0:T(8,128)S(1)}, f32[8,1024]{1,0:T(8,128)S(1)}, u32[]{:S(2)}, u32[]{:S(2)}) collective-permute-start(f32[8,1024]{1,0:T(8,128)S(1)} %get-tuple-element.22), channel_id=1, source_target_pairs={{0,25},{1,24},{2,27},{3,26},{4,29},{5,28},{6,31},{7,30},{8,17},{9,... | collective-permute-start | bytes 98312 | tf_op jit(solution)/shard_map/ppermute | solution.py:247
  13.0 2.3 %split.1 = (bf16[1024,768]{1,0:T(8,128)(2,1)S(1)}, bf16[1024,768]{1,0:T(8,128)(2,1)S(1)}) custom-call(f32[8,1024]{1,0:T(8,128)S(1)} %get-tuple-element.19.after_ref.mine_ref, f32[1024,1024]{1,0:T(8,128)} %bitcast.5), custom_call_target="tpu_custom_call" | custom-call | flops 1048576 | bytes 4194304 | tf_op jit(solution)/shard_map/split/pallas_call | solution.py:256
  15.2 0.0 collective-permute-done.5.both_ref.refs_0_
  15.3 0.8 %collective-permute-start.6 = (f32[8,1024]{1,0:T(8,128)S(1)}, f32[8,1024]{1,0:T(8,128)S(1)}, u32[]{:S(2)}, u32[]{:S(2)}) collective-permute-start(f32[8,1024]{1,0:T(8,128)S(1)} %theirs.1), channel_id=1, source_target_pairs={{0,1},{1,0},{2,3},{3,2},{4,5},{5,4},{6,7},{7,6},{8,9},{9,8},{10,11... | collective-permute-start | bytes 98312 | tf_op jit(solution)/shard_map/ppermute | solution.py:266
  16.1 0.2 collective-permute-done.4.last_ref
  16.2 0.7 %collective-permute-done.6.refs_1_ = f32[8,1024]{1,0:T(8,128)S(1)} collective-permute-done((f32[8,1024]{1,0:T(8,128)S(1)}, f32[8,1024]{1,0:T(8,128)S(1)}, u32[]{:S(2)}, u32[]{:S(2)}) %collective-permute-start.6) | collective-permute-done | bytes 32800 | tf_op jit(solution)/shard_map/ppermute | solution.py:266
  16.9 0.9 %product.1 = f32[32,8,128]{2,1,0:T(8,128)S(1)} custom-call(s32[6,128]{1,0:T(8,128)S(1)} %get-tuple-element.15.facts_ref, bf16[1024,256]{1,0:T(8,128)(2,1)S(1)} %get-tuple-element.16.high_a_ref, bf16[1024,256]{1,0:T(8,128)(2,1)S(1)} %get-tuple-element.17.low_a_ref, bf16[1024,768]{1,0:T(8,128)(2,1)S(1)} %get-tuple-element.20.after_ref.high_b_ref, ...), custom_call_target="tpu_custom_call" | custom-call | flops 201326592 | bytes 4194304 | tf_op jit(solution)/shard_map/product/pallas_call | solution.py:269
  17.8 10.5 %all_to_all.5.terms_ref = f32[32,8,128]{2,1,0:T(8,128)S(1)} all-to-all(f32[32,8,128]{2,1,0:T(8,128)S(1)} %product.1), channel_id=1, replica_groups={{0,27,22,17,12,7,2,29,24,19,14,9,4,31,26,21,16,11,6,1,28,23,18,13,8,3,3..., dimensions={0} | all-to-all | bytes 262144 | tf_op jit(solution)/shard_map/all_to_all | solution.py:279
  28.3 0.6 %resid.1 = f32[4,8,128]{2,1,0:T(8,128)} custom-call(f32[32,8,128]{2,1,0:T(8,128)S(1)} %all_to_all.5.terms_ref, f32[4,8,128]{2,1,0:T(8,128)S(1)} %get-tuple-element.24.denom_ref), custom_call_target="tpu_custom_call" | custom-call | tf_op jit(solution)/shard_map/resid/pallas_call | solution.py:287
  (1 shorter events, 0.0 us)
Async XLA Ops:
  0.0 7.4 %collective-permute-start.2 = (f32[8,1024]{1,0:T(8,128)}, f32[8,1024]{1,0:T(8,128)S(1)}, u32[]{:S(2)}, u32[]{:S(2)}) collective-permute-start(f32[8,1024]{1,0:T(8,128)} %bitcast.6), channel_id=1, source_target_pairs={{0,7},{1,6},{2,5},{3,4},{4,3},{5,2},{6,1},{7,0},{8,15},{9,14},{10,... | collective-permute-start | bytes 98312 | tf_op jit(solution)/shard_map/ppermute | solution.py:195
  3.3 4.1 %collective-permute-start.1 = (f32[8,1024]{1,0:T(8,128)}, f32[8,1024]{1,0:T(8,128)S(1)}, u32[]{:S(2)}, u32[]{:S(2)}) collective-permute-start(f32[8,1024]{1,0:T(8,128)} %bitcast.7), channel_id=1, source_target_pairs={{0,3},{1,4},{2,1},{3,6},{4,7},{5,0},{6,5},{7,2},{8,11},{9,12},{10,... | collective-permute-start | bytes 98312 | tf_op jit(solution)/shard_map/ppermute | solution.py:195
  4.2 3.9 %collective-permute-start = (f32[8,1024]{1,0:T(8,128)}, f32[8,1024]{1,0:T(8,128)S(1)}, u32[]{:S(2)}, u32[]{:S(2)}) collective-permute-start(f32[8,1024]{1,0:T(8,128)} %bitcast.8), channel_id=1, source_target_pairs={{0,5},{1,2},{2,7},{3,0},{4,1},{5,6},{6,3},{7,4},{8,13},{9,10},{10,... | collective-permute-start | bytes 98312 | tf_op jit(solution)/shard_map/ppermute | solution.py:195
  8.1 1.3 %collective-permute-start.3 = (f32[2,8,1024]{2,1,0:T(8,128)S(1)}, f32[2,8,1024]{2,1,0:T(8,128)S(1)}, u32[]{:S(2)}, u32[]{:S(2)}) collective-permute-start(f32[2,8,1024]{2,1,0:T(8,128)S(1)} %pick.1.held_ref), channel_id=1, source_target_pairs={{0,1},{1,0},{2,3},{3,2},{4,5},{5,4},{6,7},{7,6},{8,9},{9,8},{10,11... | collective-permute-start | bytes 196616 | tf_op jit(solution)/shard_map/ppermute | solution.py:232
  9.5 5.8 %collective-permute-start.5 = (f32[2,8,1024]{2,1,0:T(8,128)S(1)}, f32[2,8,1024]{2,1,0:T(8,128)S(1)}, u32[]{:S(2)}, u32[]{:S(2)}) collective-permute-start(f32[2,8,1024]{2,1,0:T(8,128)S(1)} %get-tuple-element.23), channel_id=1, source_target_pairs={{0,8},{1,17},{2,10},{3,19},{4,12},{5,21},{6,14},{7,23},{8,0},{9,25... | collective-permute-start | bytes 196616 | tf_op jit(solution)/shard_map/ppermute | solution.py:236
  11.1 5.1 %collective-permute-start.4 = (f32[8,1024]{1,0:T(8,128)S(1)}, f32[8,1024]{1,0:T(8,128)S(1)}, u32[]{:S(2)}, u32[]{:S(2)}) collective-permute-start(f32[8,1024]{1,0:T(8,128)S(1)} %get-tuple-element.22), channel_id=1, source_target_pairs={{0,25},{1,24},{2,27},{3,26},{4,29},{5,28},{6,31},{7,30},{8,17},{9,... | collective-permute-start | bytes 98312 | tf_op jit(solution)/shard_map/ppermute | solution.py:247
  15.3 1.6 %collective-permute-start.6 = (f32[8,1024]{1,0:T(8,128)S(1)}, f32[8,1024]{1,0:T(8,128)S(1)}, u32[]{:S(2)}, u32[]{:S(2)}) collective-permute-start(f32[8,1024]{1,0:T(8,128)S(1)} %theirs.1), channel_id=1, source_target_pairs={{0,1},{1,0},{2,3},{3,2},{4,5},{5,4},{6,7},{7,6},{8,9},{9,8},{10,11... | collective-permute-start | bytes 98312 | tf_op jit(solution)/shard_map/ppermute | solution.py:266
